TPU v7x, 32 devices: a whole 2x2x4 slice. The times are simulated.
32 devices in a mesh: dp: 8 (over z, core), tensor: 4 (over y, x).
Axes of the slice: x: 2, y: 2, z: 4, core: 2. Of those that a mesh axis runs over, the one named last changes fastest.
Arguments:
- tokens: bfloat16 [8192, 2048], P(('dp', 'tensor')), may hold values from -6 to 6
- attn_gain: bfloat16 [2048], P('dp'), may hold values from 0.099609375 to 1.8984375
- query_weight: bfloat16 [2048, 2048], P('dp', 'tensor'), may hold values from -0.1875 to 0.1875
- key_weight: bfloat16 [2048, 2048], P('dp', 'tensor'), may hold values from -0.125 to 0.125
- value_weight: bfloat16 [2048, 2048], P('dp', 'tensor'), may hold values from -0.125 to 0.125
- output_weight: bfloat16 [2048, 2048], P('tensor', 'dp'), may hold values from -0.75 to 0.75
- ffn_gain: bfloat16 [2048], P('dp'), may hold values from 0.099609375 to 1.8984375
- gate_weight: bfloat16 [2048, 8192], P('dp', 'tensor'), may hold values from -0.125 to 0.125
- up_weight: bfloat16 [2048, 8192], P('dp', 'tensor'), may hold values from -0.125 to 0.125
- down_weight: bfloat16 [8192, 2048], P('tensor', 'dp'), may hold values from -0.0625 to 0.0625
- cotangent: bfloat16 [8192, 2048], P(('dp', 'tensor')), may hold values from -6 to 6
Outputs:
- layer_out: bfloat16 [8192, 2048], P(('dp', 'tensor'))
- input_grad: float32 [8192, 2048], P(('dp', 'tensor'))
- attn_gain_grad: float32 [2048], P('dp')
- query_grad: float32 [2048, 2048], P('dp', 'tensor')
- key_grad: float32 [2048, 2048], P('dp', 'tensor')
- value_grad: float32 [2048, 2048], P('dp', 'tensor')
- output_grad: float32 [2048, 2048], P('tensor', 'dp')
- ffn_gain_grad: float32 [2048], P('dp')
- gate_grad: float32 [2048, 8192], P('dp', 'tensor')
- up_grad: float32 [2048, 8192], P('dp', 'tensor')
- down_grad: float32 [8192, 2048], P('tensor', 'dp')
All inputs are finite; a program needn't handle non-finite values.
Results may differ from a plain program's by a relative error of at most 0.02.
Values may be sent and summed in bfloat16 or wider, within the bound.
No kernel may reach another device: no remote copies, remote signals or barrier semaphores. Data moves between devices by JAX's collectives and lax.ppermute only.
A program may use at most 192 MiB of HBM per device.

v0:
```python
import functools

import jax
import jax.numpy as jnp
import numpy as np
from jax import lax
from jax.experimental import pallas as pl
from jax.experimental.pallas import tpu as pltpu
from jax.sharding import PartitionSpec as P

HEAD_DIM = 64
SEQ = 512
EPS = 1e-05
THETA = 130000.0
BF16 = jnp.bfloat16
F32 = jnp.float32
FACTOR = HEAD_DIM**-0.5
PAIR = 2 * HEAD_DIM
HALF_SEQ = SEQ // 2
VMEM_LIMIT = 58 << 20
COST_SHARE = 4096


class Chain:
    def __init__(self):
        self.token = jnp.zeros((8, 128), F32)
        self.swaps, self.asked = [], []

    def join(self, *values):
        *values, self.token = lax.optimization_barrier((*values, self.token))
        return values

    def gate(self, *values):
        swaps, self.swaps = self.swaps, []
        asked, self.asked = self.asked, []
        joined = self.join(
            *values, *[held[i] for held, i in swaps], *[source for source, _, _, _ in asked]
        )
        for (held, i), value in zip(swaps, joined[len(values) :]):
            held[i] = value
        for (_, held, i, swap), value in zip(asked, joined[len(values) + len(swaps) :]):
            held[i] = swap(value)
            self.swaps.append((held, i))
        return joined[: len(values)]

    def end(self, *transfers):
        counts = [len(t.flying) for t in transfers]
        got = self.gate(*[value for t in transfers for value in t.flying])
        for t, count in zip(transfers, counts):
            if count:
                t.go_on(got[:count])
            got = got[count:]

    def ask(self, source, held, i, swap):
        self.asked.append((source, held, i, swap))

    def flush(self):
        for source, held, i, swap in self.asked:
            held[i] = swap(source)
        self.asked = []

    def call(self, body, grid, ins, outs, shapes, flops, scratch=(), prefetch=0, moved=0):
        first = prefetch + len(ins)
        second = first + 1 + len(outs)
        anywhere = pl.BlockSpec(memory_space=pl.ANY)

        def wrapped(*refs):
            body(*refs[:first], *refs[first + 1 : second], *refs[second + 1 :])

        run = pl.pallas_call(
            wrapped,
            grid_spec=pltpu.PrefetchScalarGridSpec(
                num_scalar_prefetch=prefetch,
                grid=grid,
                in_specs=[*ins, anywhere],
                out_specs=[*outs, anywhere],
                scratch_shapes=list(scratch),
            ),
            out_shape=[jax.ShapeDtypeStruct(s, t) for s, t in [*shapes, ((8, 128), F32)]],
            compiler_params=pltpu.CompilerParams(
                vmem_limit_bytes=VMEM_LIMIT, dimension_semantics=("arbitrary",) * len(grid)
            ),
            cost_estimate=pl.CostEstimate(
                flops=flops // COST_SHARE, bytes_accessed=moved // COST_SHARE, transcendentals=0
            ),
        )

        def with_token(*args):
            *results, self.token = run(*args, self.token)
            return results

        return with_token


class Chips:
    def __init__(self, size):
        self.bits = (size // 2).bit_length() - 1
        self.size = size
        self.swap = [(i, i ^ 1) for i in range(size)]
        self.links = [
            [(i, i ^ 2 << self.bits - 1 - p) for i in range(size)] for p in range(self.bits)
        ]
        flips = [
            sum(1 << self.bits - 1 - p for p in range(self.bits) if v >> p & 1)
            for v in range(1 << self.bits)
        ]
        table = [[i ^ 2 * f for f in flips] + [i ^ 2 * f ^ 1 for f in flips] for i in range(size)]
        self.table = np.array(table, np.int32)

    def send(self, value, p):
        return lax.ppermute(value, "dp", self.links[p])

    def other(self, value):
        return lax.ppermute(value, "dp", self.swap)


class Gather:
    def __init__(self, chips, chain, piece):
        self.chips, self.chain = chips, chain
        self.own = [piece] + [None] * (2**chips.bits - 1)
        self.others = list(self.own)
        self.ask(0)
        self.keys = [1 << p for p in range(chips.bits)]
        self.flying = [chips.send(piece, p) for p in range(chips.bits)]

    def ask(self, v):
        self.chain.ask(self.own[v], self.others, v, self.chips.other)

    def go_on(self, got):
        keys, self.keys, self.flying = self.keys, [], []
        for v, piece in zip(keys, got):
            self.own[v] = piece
            for p in range(v.bit_length(), self.chips.bits):
                self.keys.append(v | 1 << p)
                self.flying.append(self.chips.send(piece, p))
        for v in keys:
            self.ask(v)

    def pieces(self):
        while self.flying:
            self.chain.end(self)
        self.chain.flush()
        return self.own + self.others


class Sums:
    def __init__(self, chips, chain, mine, apart=False, hold=False, cut_in_two=False):
        self.chips, self.chain, self.apart, self.hold = chips, chain, apart, hold
        self.todo = []
        self.cut_in_two = cut_in_two and chips.bits == 2
        self.parts = [mine[0]]
        mine = list(mine[1:])
        self.direct, self.passed = [], []
        for p in range(chips.bits):
            self.direct.append(mine.pop(0))
            self.passed.append(mine.pop(0) if p else None)
        self.p = chips.bits - 1
        if self.cut_in_two:
            self.kinds = [0, 1]
            self.flying = [chips.send(half, 1) for half in self.in_two(self.passed[1])]
            return
        self.kinds = [self.p]
        self.flying = [chips.send(self.passed[self.p], self.p)]

    def in_two(self, values):
        width = values.shape[1] // 2
        return values[:, :width], values[:, width:]

    def go_on(self, got):
        rows = self.parts[0].shape[0]
        kinds, self.kinds, self.flying = self.kinds, [], []
        if self.p == 0:
            self.parts += got
            return
        if self.cut_in_two:
            self.p = 0
            total = self.direct[0].astype(F32) + jnp.concatenate(got, axis=1).astype(F32)
            self.todo = [(None, self.direct[1], 1), (None, total.astype(BF16), 0)]
            self.resume()
            return
        for kind, block in zip(kinds, got):
            if kind is None:
                self.parts.append(block)
                continue
            add = lambda held, first: (
                held.astype(F32) + block[first * rows : first * rows + held.shape[0]].astype(F32)
            ).astype(BF16)
            for q in range(kind):
                self.direct[q] = add(self.direct[q], (1 << q) - 1)
                if q:
                    self.passed[q] = add(self.passed[q], 1 << q)
        p, self.p = self.p, self.p - 1
        if p > 0:
            self.todo.append((None, self.direct[p], p))
        if p > 1:
            self.todo.append((p - 1, self.passed[p - 1], p - 1))
        if p == 1 and not self.apart:
            self.todo.append((None, self.direct[0], 0))
        if not self.hold:
            self.resume()

    def resume(self):
        todo, self.todo = self.todo, []
        values = self.chain.join(*[value for _, value, _ in todo])
        for (kind, _, p), value in zip(todo, values):
            self.kinds.append(kind)
            self.flying.append(self.chips.send(value, p))

    def send_half(self, i):
        while self.p > 0:
            self.chain.end(self)
        width = self.direct[0].shape[1] // 2
        (value,) = self.chain.join(self.direct[0][:, i * width : (i + 1) * width])
        self.kinds.append(None)
        self.flying.append(self.chips.send(value, 0))

    def terms(self):
        while self.flying or self.todo:
            if self.todo:
                self.resume()
            self.chain.end(self)
        return sorted(self.parts, key=lambda part: -part.shape[1])


class Group:
    def __init__(self, links, axes):
        self.links, self.axes = links, axes
        self.bits = len(links)
        self.size = 1 << self.bits
        self.orders = (list(range(self.bits)), list(range(self.bits))[::-1])

    def send(self, value, bit):
        return lax.ppermute(value, self.axes, self.links[bit])

    def messages(self):
        found = []
        for order in self.orders:
            found.append([])
            for top in reversed(range(self.bits)):
                found[-1].append(
                    [
                        1 << order[top] | sum(1 << order[p] for p in range(top) if v >> p & 1)
                        for v in range(1 << top)
                    ]
                )
        return found


class Spread:
    def __init__(self, group, chain, rows):
        self.group, self.chain = group, chain
        self.held = {0: [rows]}
        self.later = None
        self.keys = [(1 << b, None) for b in range(group.bits)]
        self.flying = [group.send(rows, b) for b in range(group.bits)]

    def go_on(self, got):
        fresh = list(zip(self.keys, got))
        self.keys, self.flying = [], []
        for (k, h), block in fresh:
            if h is None:
                self.held[k] = [block]
            else:
                self.held.setdefault(k, [None, None])[h] = block
        for (k, h), block in fresh:
            for way, order in enumerate(self.group.orders):
                if h is not None and h != way:
                    continue
                half = block.shape[1] // 2
                top = max(i for i, bit in enumerate(order) if k >> bit & 1)
                for i in range(top + 1, len(order)):
                    part = block if h is not None else block[:, way * half : (way + 1) * half]
                    self.keys.append((k | 1 << order[i], way))
                    if self.later is not None:
                        self.later.append((part, order[i]))
                    else:
                        self.flying.append(self.group.send(part, order[i]))

        if self.later:
            parts = self.chain.join(*[part for part, _ in self.later])
            self.later = [(part, bit) for part, (_, bit) in zip(parts, self.later)]

    def resume(self):
        later, self.later = self.later, None
        parts = self.chain.join(*[part for part, _ in later])
        self.flying = [self.group.send(part, bit) for part, (_, bit) in zip(parts, later)]

    def blocks(self):
        while self.flying:
            self.chain.end(self)
        return [self.held[k] for k in range(self.group.size)]


class Fold:
    def __init__(self, group, chain, own, sent):
        self.group, self.chain = group, chain
        self.rows = own[0].shape[0]
        self.sent = [list(half) for half in sent]
        self.parts = [[half] for half in own]
        self.wave = 0
        self.start()

    def start(self):
        self.flying = [
            self.group.send(self.sent[h][self.wave], order[self.group.bits - 1 - self.wave])
            for h, order in enumerate(self.group.orders)
        ]

    def go_on(self, got):
        self.wave += 1
        self.flying = []
        for h, block in enumerate(got):
            self.parts[h].append(block)
        for wave in range(self.wave, self.group.bits):
            sums = add_rows(self.chain, [sent[wave] for sent in self.sent], got)
            for sent, value in zip(self.sent, sums):
                sent[wave] = value
        if self.wave < self.group.bits:
            self.start()

    def total(self):
        while self.flying:
            self.chain.end(self)
        return self.parts


class Weight:
    def __init__(self, pieces, rows, start, width):
        self.pieces, self.rows, self.start, self.width = pieces, rows, start, width
        self.model = len(pieces) * rows

    def tiles(self, tile):
        first = self.start // tile
        return [pl.BlockSpec((self.rows, tile), lambda j: (0, first + j))] * len(self.pieces)


def nn(left, right):
    return lax.dot_general(left, right, (((1,), (0,)), ((), ())), preferred_element_type=F32)


def nt(left, right):
    return lax.dot_general(left, right, (((1,), (1,)), ((), ())), preferred_element_type=F32)


def tn(left, right):
    return lax.dot_general(left, right, (((0,), (0,)), ((), ())), preferred_element_type=F32)


def whole(shape):
    return pl.BlockSpec(shape, lambda *_: (0,) * len(shape))


def place(line_ref, j, width):
    return pl.ds(pl.multiple_of(line_ref[j] * width, 128), width)


def cut(width, j):
    return slice(j * width, (j + 1) * width)


def scale_of(values):
    return lax.rsqrt(jnp.mean(values * values, axis=-1, keepdims=True) + EPS)


def fetch_blocks(counts, refs, held, sems, k, slot, wait):
    first = 0
    for i, count in enumerate(counts):
        copies = []
        half = held.shape[2] // count
        for h in range(count):
            target = held.at[slot, :, pl.ds(h * half, half)]
            copies.append(pltpu.make_async_copy(refs[first + h], target, sems.at[slot, h]))
        first += count

        @pl.when(k == i)
        def _():
            for copy in copies:
                copy.wait() if wait else copy.start()


def fetched(counts, refs, held, sems):
    k = pl.program_id(0)

    @pl.when(k == 0)
    def _():
        fetch_blocks(counts, refs, held, sems, k, 0, False)

    fetch_blocks(counts, refs, held, sems, k + 1, (k + 1) % 2, False)
    fetch_blocks(counts, refs, held, sems, k, k % 2, True)
    return held.at[k % 2]


def norm_body(blocks, counts, line_ref, gain_ref, *refs):
    out_ref, held, sems = refs[sum(counts) :]
    x_ref = fetched(counts, refs, held, sems)
    width = out_ref.shape[1] // blocks
    scale = scale_of(x_ref[...].astype(F32))
    for j in range(blocks):
        part = x_ref[:, place(line_ref, j, width)].astype(F32)
        gain = gain_ref[0:1, cut(width, j)]
        out_ref[:, cut(width, j)] = (part * scale * gain).astype(BF16)


def order_body(blocks, counts, line_ref, gain_ref, *refs):
    out_ref, held, sems = refs[sum(counts) :]
    x_ref = fetched(counts, refs, held, sems)
    width = out_ref.shape[1] // blocks
    for j in range(blocks):
        out_ref[:, cut(width, j)] = x_ref[:, place(line_ref, j, width)]


def ordered(chain, body, line, gains, held):
    counts = [len(block) for block in held]
    rows, model = held[0][0].shape
    n = len(held)
    return chain.call(
        functools.partial(body, line.shape[0], counts),
        (n,),
        [whole(gains.shape)] + [pl.BlockSpec(memory_space=pl.ANY)] * sum(counts),
        [pl.BlockSpec((rows, model), lambda k, *_: (k, 0))],
        [((n * rows, model), BF16)],
        flops=20 * n * rows * model,
        scratch=[pltpu.VMEM((2, rows, model), BF16), pltpu.SemaphoreType.DMA((2, 2))],
        prefetch=1,
        moved=4 * n * rows * model,
    )(line, gains, *[array for block in held for array in block])[0]


def added(refs, span):
    total = refs[0][span, :].astype(F32)
    for ref in refs[1:]:
        total += ref[span, :].astype(F32)
    return total


def middle_body(blocks, m, line_ref, x_ref, gain_ref, *refs):
    middle_ref, out_ref = refs[2 * m :]
    width = x_ref.shape[1] // blocks
    half = x_ref.shape[1] // 2
    span = slice(None)
    middle_ref[:, :half] = added(refs[:m], span)
    middle_ref[:, half:] = added(refs[m : 2 * m], span)
    for j in range(blocks):
        here = x_ref[:, place(line_ref, j, width)].astype(F32)
        middle_ref[:, cut(width, j)] += here
    middle = middle_ref[...]
    out_ref[...] = (middle * scale_of(middle) * gain_ref[1:2, :]).astype(BF16)


def result_body(blocks, m, line_ref, middle_ref, gain_ref, *refs):
    out_ref = refs[2 * m]
    width = middle_ref.shape[1] // blocks
    span = slice(None)
    total = middle_ref[...] + jnp.concatenate(
        [added(refs[:m], span), added(refs[m : 2 * m], span)], axis=1
    )
    for j in range(blocks):
        out_ref[:, place(line_ref, j, width)] = total[:, cut(width, j)].astype(BF16)


def second_back_body(blocks, m, line_ref, dy_ref, gain_ref, *refs):
    middle_ref, out_ref, low_ref = refs[2 * m :]
    width = dy_ref.shape[1] // blocks
    span = slice(None)
    grad = jnp.concatenate([added(refs[:m], span), added(refs[m : 2 * m], span)], axis=1)
    middle = middle_ref[...]
    scale = scale_of(middle)
    normed = middle * scale
    scaled = grad * gain_ref[1:2, :]
    out_ref[...] = scale * (scaled - normed * jnp.mean(scaled * normed, axis=-1, keepdims=True))
    for j in range(blocks):
        out_ref[:, cut(width, j)] += dy_ref[:, place(line_ref, j, width)].astype(F32)
    low_ref[...] = out_ref[...].astype(BF16)


def first_back_body(blocks, m, line_ref, x_ref, gain_ref, *refs):
    above_ref, out_ref = refs[2 * m :]
    width = x_ref.shape[1] // blocks
    span = slice(None)
    scale = scale_of(x_ref[...].astype(F32))
    normed = jnp.concatenate(
        [x_ref[:, place(line_ref, j, width)].astype(F32) for j in range(blocks)], axis=1
    ) * scale
    grad = jnp.concatenate([added(refs[:m], span), added(refs[m : 2 * m], span)], axis=1)
    scaled = grad * gain_ref[0:1, :]
    back = scale * (scaled - normed * jnp.mean(scaled * normed, axis=-1, keepdims=True))
    total = above_ref[...] + back
    for j in range(blocks):
        out_ref[:, place(line_ref, j, width)] = total[:, cut(width, j)]


def by_rows(chain, body, line, first, gains, parts, more, kinds):
    rows, model = first.shape
    half = model // 2
    tile = min(128, rows)
    row = pl.BlockSpec((tile, model), lambda i, *_: (i, 0))
    slim = pl.BlockSpec((tile, half), lambda i, *_: (i, 0))
    m = len(parts[0])
    return chain.call(
        functools.partial(body, line.shape[0], m),
        (rows // tile,),
        [row, whole(gains.shape)] + [slim] * (2 * m) + [row] * len(more),
        [row] * len(kinds),
        [((rows, model), kind) for kind in kinds],
        flops=20 * rows * model,
        prefetch=1,
        moved=rows * model * (2 * m + 4 * len(kinds)),
    )(line, first, gains, *parts[0], *parts[1], *more)


def add_rows_body(count, *refs):
    for i in range(count):
        total = refs[i][...].astype(F32) + refs[count + i][...].astype(F32)
        refs[2 * count + i][...] = total.astype(BF16)


def add_rows(chain, helds, blocks):
    rows, columns = helds[0].shape
    tile = min(128, rows)
    steps = rows // tile
    count = len(helds)
    here = pl.BlockSpec((tile, columns), lambda i: (i, 0))
    return chain.call(
        functools.partial(add_rows_body, count),
        (steps,),
        [here] * count + [pl.BlockSpec((tile, columns), lambda i: (steps + i, 0))] * count,
        [here] * count,
        [((rows, columns), BF16)] * count,
        flops=count * rows * columns,
        moved=6 * count * rows * columns,
    )(*helds, *blocks)


def finish_body(m, halves, n, *refs):
    total = added(refs[:m], slice(None))
    if halves:
        total += jnp.concatenate([ref[...].astype(F32) for ref in refs[m : m + halves]], axis=1)
    m += halves
    weights, outs = refs[m : m + n], refs[m + n :]
    if not n:
        outs[0][...] = total.T
        return
    width = weights[0].shape[1]
    inner = jnp.zeros((total.shape[0], 1), F32)
    for i in range(n):
        part = total[:, cut(width, i)]
        outs[i][...] = part
        inner += jnp.sum(weights[i][...].astype(F32) * part, axis=1, keepdims=True)
    outs[n][...] = jnp.broadcast_to(inner, outs[n].shape)


def finish(chain, terms, weights=()):
    rows, columns = terms[0].shape
    tile = min(128, rows)
    row = pl.BlockSpec((tile, columns), lambda i: (i, 0))
    n = len(weights)
    halves = sum(1 for term in terms if term.shape[1] < columns)
    half = [pl.BlockSpec((tile, columns // 2), lambda i: (i, 0))] * halves
    if n:
        slim = pl.BlockSpec((tile, columns // n), lambda i: (i, 0))
        outs = [slim] * n + [pl.BlockSpec((tile, 128), lambda i: (i, 0))]
        shapes = [((rows, columns // n), F32)] * n + [((rows, 128), F32)]
    else:
        slim = None
        outs = [pl.BlockSpec((columns, tile), lambda i: (0, i))]
        shapes = [((columns, rows), F32)]
    results = chain.call(
        functools.partial(finish_body, len(terms) - halves, halves, n),
        (rows // tile,),
        [row] * (len(terms) - halves) + half + [slim] * n,
        outs,
        shapes,
        flops=4 * rows * columns,
        moved=rows * columns * 12,
    )(*terms, *weights)
    if n:
        results[n] = results[n][:, 0]
    return results


def rope_tables(place):
    half = HEAD_DIM // 2
    freq = THETA ** (-2.0 * jnp.arange(half, dtype=F32) / HEAD_DIM)
    angle = place.astype(F32)[:, None] * freq[None, :]
    cosine, sine = jnp.cos(angle), jnp.sin(angle)
    return (
        jnp.concatenate([cosine] * (PAIR // half), axis=1),
        jnp.concatenate([-sine, sine] * (PAIR // HEAD_DIM), axis=1),
    )


def turn(values):
    half = HEAD_DIM // 2
    width = values.shape[-1]
    lane = lax.broadcasted_iota(jnp.int32, values.shape, 1) % HEAD_DIM
    return jnp.where(
        lane < half, pltpu.roll(values, width - half, 1), pltpu.roll(values, half, 1)
    )


def joined(refs):
    return jnp.concatenate([r[...] for r in refs], axis=0)


def qkv_body(n, x_ref, cos_ref, sin_ref, *refs):
    weights, outs = refs[: 3 * n], refs[3 * n :]
    rows = x_ref.shape[0]
    tile = outs[0].shape[1]
    for i in range(3):
        weight = joined(weights[i * n : (i + 1) * n])
        for s in range(rows // SEQ):
            span = slice(s * SEQ, (s + 1) * SEQ)
            product = nn(x_ref[span, :], weight)
            if i == 2:
                outs[i][span, :] = product.astype(BF16)
                continue
            for t in range(tile // PAIR):
                here = product[:, t * PAIR : (t + 1) * PAIR]
                turned = here * cos_ref[...] + turn(here) * sin_ref[...]
                outs[i][span, t * PAIR : (t + 1) * PAIR] = turned.astype(BF16)


def project(chain, x, tables, query, key, value):
    rows, model = x.shape
    n, width = len(query.pieces), query.width
    tile = min(256, width)
    out = pl.BlockSpec((rows, tile), lambda j: (0, j))
    return chain.call(
        functools.partial(qkv_body, n),
        (width // tile,),
        [whole(x.shape), whole((SEQ, PAIR)), whole((SEQ, PAIR))]
        + query.tiles(tile)
        + key.tiles(tile)
        + value.tiles(tile),
        [out] * 3,
        [((rows, width), BF16)] * 3,
        flops=6 * rows * model * width,
        moved=2 * (rows * model + 3 * model * width + 3 * rows * width),
    )(x, *tables, *query.pieces, *key.pieces, *value.pieces)


def collect(counts, refs, held, sems):
    rows = held.shape[0] // len(counts)
    copies = []
    for k, count in enumerate(counts):
        half = held.shape[1] // count
        for h in range(count):
            target = held.at[pl.ds(k * rows, rows), pl.ds(h * half, half)]
            i = len(copies)
            copies.append(pltpu.make_async_copy(refs[i], target, sems.at[i]))
    for copy in copies:
        copy.start()
    for copy in copies:
        copy.wait()


def gate_body(n, counts, *refs):
    m = sum(counts)
    gate_w, up_w = refs[m : m + n], refs[m + n : m + 2 * n]
    left_ref, hidden_ref, slope_ref, silu_ref, theirs_ref, x_ref, turned, sems = refs[m + 2 * n :]

    @pl.when(pl.program_id(0) == 0)
    def _():
        collect(counts, refs, x_ref, sems)
        turned[...] = left_ref[...].T

    gate_weight, up_weight = joined(gate_w), joined(up_w)
    for s in range(x_ref.shape[0] // SEQ):
        span = slice(s * SEQ, (s + 1) * SEQ)
        gate = nn(x_ref[span, :], gate_weight)
        up = nn(x_ref[span, :], up_weight)
        sigm = jax.nn.sigmoid(gate)
        silu = gate * sigm
        hidden_ref[span, :] = (silu * up).astype(BF16)
        silu_ref[span, :] = silu.astype(BF16)
        slope_ref[span, :] = (up * sigm * (1.0 + gate * (1.0 - sigm))).astype(BF16)
    theirs_ref[...] = nn(turned[...], hidden_ref[...]).astype(BF16)


def collected(held):
    counts = [len(block) for block in held]
    rows, model = held[0][0].shape
    scratch = [
        pltpu.VMEM((len(held) * rows, model), BF16),
        pltpu.SemaphoreType.DMA((sum(counts),)),
    ]
    arrays = [array for block in held for array in block]
    return counts, arrays, [pl.BlockSpec(memory_space=pl.ANY)] * len(arrays), scratch


def gate_up(chain, held, gate, up, grads):
    counts, arrays, specs, scratch = collected(held)
    rows, model = scratch[0].shape
    n, width = len(gate.pieces), gate.width
    tile = min(256, width)
    out = pl.BlockSpec((rows, tile), lambda j: (0, j))
    half = model // 2
    return chain.call(
        functools.partial(gate_body, n, counts),
        (width // tile,),
        specs
        + gate.tiles(tile)
        + up.tiles(tile)
        + [pl.BlockSpec((rows, half), lambda j: (0, 1))],
        [out] * 3 + [pl.BlockSpec((half, tile), lambda j: (0, j))],
        [((rows, width), BF16)] * 3 + [((half, width), BF16)],
        flops=6 * rows * model * width,
        scratch=[scratch[0], pltpu.VMEM((half, rows), BF16), scratch[1]],
        moved=2 * (rows * model + 2 * model * width + 3 * rows * width),
    )(*arrays, *gate.pieces, *up.pieces, grads)


def half_blocks(left, which):
    lefts = [block[0] if len(block) == 1 else block[which] for block in left]
    rows, half = lefts[0].shape[0], left[0][0].shape[1] // 2
    places = [which if len(block) == 1 else 0 for block in left]
    return lefts, [
        pl.BlockSpec((rows, half), functools.partial(lambda at, j: (0, at), at)) for at in places
    ]


def hidden_back_body(n, blocks, g_ref, *refs):
    weights, slope_ref, silu_ref = refs[:n], refs[n], refs[n + 1]
    lefts, refs = refs[n + 2 : n + 2 + blocks], refs[n + 2 + blocks :]
    gate_ref, up_ref, theirs_ref, turned = refs
    rows = turned.shape[1] // blocks

    @pl.when(pl.program_id(0) == 0)
    def _():
        for k in range(blocks):
            turned[:, cut(rows, k)] = lefts[k][...].T

    weight = joined(weights)
    for s in range(g_ref.shape[0] // SEQ):
        span = slice(s * SEQ, (s + 1) * SEQ)
        grad = nn(g_ref[span, :], weight)
        gate_ref[span, :] = (grad * slope_ref[span, :].astype(F32)).astype(BF16)
        up_ref[span, :] = (grad * silu_ref[span, :].astype(F32)).astype(BF16)
    theirs_ref[...] = nn(turned[...], gate_ref[...]).astype(BF16)


def hidden_back(chain, grads, down, slope, silu, left):
    rows, model = grads.shape
    n, width = len(down.pieces), down.width
    tile = min(256, width)
    out = pl.BlockSpec((rows, tile), lambda j: (0, j))
    lefts, specs = half_blocks(left, 1)
    half = model // 2
    return chain.call(
        functools.partial(hidden_back_body, n, len(lefts)),
        (width // tile,),
        [whole(grads.shape)] + down.tiles(tile) + [out] * 2 + specs,
        [out] * 2 + [pl.BlockSpec((half, tile), lambda j: (0, j))],
        [((rows, width), BF16)] * 2 + [((half, width), BF16)],
        flops=3 * rows * model * width,
        scratch=[pltpu.VMEM((half, rows), BF16)],
        moved=2 * (rows * model + model * width + 4 * rows * width),
    )(grads, *down.pieces, slope, silu, *lefts)


def mixed_back_body(n, counts, *refs):
    m = sum(counts)
    out_ref, x_ref, sems = refs[m + n :]

    @pl.when(pl.program_id(0) == 0)
    def _():
        collect(counts, refs, x_ref, sems)

    out_ref[...] = nn(x_ref[...], joined(refs[m : m + n])).astype(BF16)


def mixed_back(chain, held, out):
    counts, arrays, specs, scratch = collected(held)
    rows, model = scratch[0].shape
    n, width = len(out.pieces), out.width
    tile = min(256, width)
    return chain.call(
        functools.partial(mixed_back_body, n, counts),
        (width // tile,),
        specs + out.tiles(tile),
        [pl.BlockSpec((rows, tile), lambda j: (0, j))],
        [((rows, width), BF16)],
        flops=2 * rows * model * width,
        scratch=scratch,
        moved=2 * (rows * model + model * width + rows * width),
    )(*arrays, *out.pieces)[0]


def trans_body(n, starts, targets, chunks, *refs):
    parts, blocks = len(starts), len(targets[0])
    arrays = refs[:parts]
    pieces, outs = refs[parts : parts * (n + 1)], refs[parts * (n + 1) : -6]
    lefts, held, ready, left_sems, sems, out_sems = refs[-6:]
    j = pl.program_id(0)
    depth, width = held.shape[2:]
    rows = ready.shape[1] // blocks
    chunk = width // chunks

    def left_copy(p, c):
        span = pl.ds(c * chunk, chunk)
        return pltpu.make_async_copy(
            arrays[p].at[:, span], lefts.at[p, :, span], left_sems.at[p, c]
        )

    def copy(i, p, slot):
        source = pieces[p * n + i].at[pl.ds(0, depth), pl.ds(starts[p], width)]
        return pltpu.make_async_copy(source, held.at[slot, p], sems.at[slot, p])

    def fetch(step, slot):
        for i in range(n):

            @pl.when(step == i)
            def _():
                for p in range(parts):
                    copy(i, p, slot).start()

    def leave(slot, k, array, first, column):
        target = outs[array].at[pl.ds(first, rows), pl.ds(column, depth)]
        source = ready.at[slot, pl.ds(k * rows, rows), :]
        return pltpu.make_async_copy(source, target, out_sems.at[slot, k])

    def left(slot):
        for k in range(blocks):
            leave(slot, k, 0, 0, 0).wait()

    @pl.when(j == 0)
    def _():
        fetch(j, 0)
        for c in range(chunks):
            for p in range(parts):
                left_copy(p, c).start()

    @pl.when(j + 1 < n)
    def _():
        fetch(j + 1, (j + 1) % 2)

    slot = j % 2
    for p in range(parts):
        copy(0, p, slot).wait()

    @pl.when(j >= 2)
    def _():
        left(slot)

    spans = [slice(s * SEQ, (s + 1) * SEQ) for s in range(blocks * rows // SEQ)]

    @pl.when(j == 0)
    def _():
        totals = [None] * len(spans)
        for c in range(chunks):
            for p in range(parts):
                left_copy(p, c).wait()
                for s, span in enumerate(spans):
                    part = nt(lefts[p, span, cut(chunk, c)], held[0, p, :, cut(chunk, c)])
                    totals[s] = part if totals[s] is None else totals[s] + part
        for total, span in zip(totals, spans):
            ready[0, span, :] = total.astype(BF16)

    @pl.when(j > 0)
    def _():
        for span in spans:
            total = nt(lefts[0, span, :], held[slot, 0])
            for p in range(1, parts):
                total += nt(lefts[p, span, :], held[slot, p])
            ready[slot, span, :] = total.astype(BF16)

    column = pl.multiple_of(j % (n // 2) * depth, 128)
    for h in range(2):

        @pl.when((j >= n // 2) == (h == 1))
        def _():
            for k, (array, first) in enumerate(targets[h]):
                leave(slot, k, array, first, column).start()

    @pl.when(j == n - 1)
    def _():
        left(1 - slot)
        left(slot)


def times_trans(chain, parts, group):
    weights = [weight for _, weight in parts]
    n, depth, width = len(weights[0].pieces), weights[0].rows, weights[0].width
    rows = parts[0][0].shape[0]
    half = weights[0].model // 2
    size = rows // group.size
    messages = group.messages()
    shapes = [((size, half), BF16)] * 2
    targets = [{0: (0, 0)}, {0: (1, 0)}]
    for h in range(2):
        for keys in messages[h]:
            for i, k in enumerate(keys):
                targets[h][k] = (len(shapes), i * size)
            shapes.append(((len(keys) * size, half), BF16))
    targets = [[t[k] for k in range(group.size)] for t in targets]
    anywhere = pl.BlockSpec(memory_space=pl.ANY)
    chunks = max(1, width // 512)
    outs = chain.call(
        functools.partial(trans_body, n, [weight.start for weight in weights], targets, chunks),
        (n,),
        [anywhere] * ((n + 1) * len(parts)),
        [anywhere] * len(shapes),
        shapes,
        flops=4 * rows * half * width * len(parts),
        scratch=[
            pltpu.VMEM((len(parts), rows, width), BF16),
            pltpu.VMEM((2, len(parts), depth, width), BF16),
            pltpu.VMEM((2, rows, depth), BF16),
            pltpu.SemaphoreType.DMA((len(parts), chunks)),
            pltpu.SemaphoreType.DMA((2, len(parts))),
            pltpu.SemaphoreType.DMA((2, group.size)),
        ],
        moved=2 * (2 * rows * half + len(parts) * (rows + 2 * half) * width),
    )(*[left for left, _ in parts], *[piece for weight in weights for piece in weight.pieces])
    m = group.bits
    return outs[:2], [outs[2 : 2 + m], outs[2 + m :]]


def grad_body(parts, got, blocks, steps, *refs):
    lefts, refs = refs[:blocks], refs[blocks:]
    rights, refs = refs[:parts], refs[parts:]
    got_ref = refs[0] if got else None
    outs, turned = refs[got:-1], refs[-1]
    j = pl.program_id(0)

    @pl.when(j == 0)
    def _():
        rows = turned.shape[1] // blocks
        for k in range(blocks):
            turned[:, cut(rows, k)] = lefts[k][...].T

    for i in range(parts):

        @pl.when((j >= i * steps) & (j < (i + 1) * steps))
        def _():
            total = nn(turned[...], rights[i][...])
            if got:
                total += got_ref[...].astype(F32)
            total = total.astype(BF16)
            first = 0
            for out_ref in outs:
                count = out_ref.shape[0]
                out_ref[...] = total[first : first + count]
                first += count


def weight_grads(chain, left, which, rights, got=None, bits=0):
    rows, width = rights[0].shape
    parts = len(rights)
    tile = min(512, width)
    steps = width // tile
    lefts, ins = half_blocks(left if isinstance(left, list) else [[left]], which)
    blocks, half = len(lefts), ins[0].block_shape[1]
    for i in range(parts):
        ins.append(
            pl.BlockSpec(
                (rows, tile),
                functools.partial(
                    lambda first, j: (0, jnp.clip(j - first, 0, steps - 1)), i * steps
                ),
            )
        )
    column = lambda j: (0, j)
    more = [] if got is None else [got]
    sizes = [half >> bits]
    for p in range(bits):
        sizes += [sizes[0], ((1 << p) - 1) * sizes[0]] if p else [sizes[0]]
    return chain.call(
        functools.partial(grad_body, parts, len(more), blocks, steps),
        (parts * steps,),
        ins + [pl.BlockSpec((half, tile), column)] * len(more),
        [pl.BlockSpec((size, tile), column) for size in sizes],
        [((size, parts * width), BF16) for size in sizes],
        flops=2 * rows * half * width * parts,
        scratch=[pltpu.VMEM((half, rows), BF16)],
        moved=2 * (rows * half + parts * (rows + half) * width),
    )(*lefts, *rights, *more)


def causal(scores):
    past = scores.shape[0] - HALF_SEQ
    key = lax.broadcasted_iota(jnp.int32, (HALF_SEQ, HALF_SEQ), 0)
    query = lax.broadcasted_iota(jnp.int32, (HALF_SEQ, HALF_SEQ), 1)
    last = jnp.where(key <= query, scores[past:], -1e30)
    return last if past == 0 else jnp.concatenate([scores[:past], last], axis=0)


def head_of(h):
    return slice(h * HEAD_DIM, (h + 1) * HEAD_DIM)


def span_of(b):
    return slice(b * HALF_SEQ, (b + 1) * HALF_SEQ)


def in_place(shift_ref, ref, count):
    rows = SEQ // count
    spans = [pl.ds(pl.multiple_of((i ^ shift_ref[0]) * rows, rows), rows) for i in range(count)]
    return jnp.concatenate([ref[span, :] for span in spans], axis=0)


def put_back(shift_ref, ref, count, values):
    rows = SEQ // count
    for i in range(count):
        ref[pl.ds(pl.multiple_of((i ^ shift_ref[0]) * rows, rows), rows), :] = values[cut(rows, i)]


def one_head(values, h):
    lane = lax.broadcasted_iota(jnp.int32, values.shape, 1)
    return jnp.where(lane // HEAD_DIM == h, values, jnp.zeros_like(values))


def attend_body(count, shift_ref, q_ref, k_ref, v_ref, out_ref, sum_ref):
    queries, keys = in_place(shift_ref, q_ref, count), in_place(shift_ref, k_ref, count)
    values = in_place(shift_ref, v_ref, count).astype(F32).T.astype(BF16)
    heads = []
    for h in range(q_ref.shape[1] // HEAD_DIM):
        blocks = []
        for b in range(2):
            reach = (b + 1) * HALF_SEQ
            query = one_head(queries[span_of(b)] * BF16(FACTOR), h)
            scores = causal(nt(keys[:reach], query))
            top = jnp.max(scores, axis=0, keepdims=True)
            expo = jnp.exp(scores - top)
            total = jnp.sum(expo, axis=0, keepdims=True)
            mixed = nn(values[head_of(h), :reach], expo.astype(BF16))
            blocks.append(mixed * (1.0 / total))
            sum_ref[0, h, :, span_of(b)] = top + jnp.log(total)
        heads.append(jnp.concatenate(blocks, axis=1))
    put_back(shift_ref, out_ref, count, jnp.concatenate(heads, axis=0).T.astype(BF16))


def attention_specs(rows, width, wide):
    wide = min(wide, width)
    tile = pl.BlockSpec((SEQ, wide), lambda s, p, _: (s, p))
    sums = pl.BlockSpec((1, wide // HEAD_DIM, 1, SEQ), lambda s, p, _: (s, p, 0, 0))
    return (rows // SEQ, width // wide), tile, sums


def attend(chain, shift, count, query, key, value):
    rows, width = query.shape
    grid, tile, sums = attention_specs(rows, width, 256)
    return chain.call(
        functools.partial(attend_body, count),
        grid,
        [tile] * 3,
        [tile, sums],
        [((rows, width), BF16), ((rows // SEQ, width // HEAD_DIM, 1, SEQ), F32)],
        flops=16 * rows * width * SEQ,
        prefetch=1,
        moved=8 * rows * width,
    )(shift, query, key, value)


def attend_back_body(
    count, shift_ref, q_ref, k_ref, v_ref, g_ref, sum_ref, cos_ref, sin_ref, dq_ref, dk_ref, dv_ref
):
    queries, keys, values, grads = (
        in_place(shift_ref, ref, count) for ref in (q_ref, k_ref, v_ref, g_ref)
    )
    turned = keys.astype(F32).T.astype(BF16)
    dq_heads = []
    dk, dv = [], []
    for b in range(2):
        reach = (b + 1) * HALF_SEQ
        dq, dk_sum, dv_sum = [], None, None
        for h in range(q_ref.shape[1] // HEAD_DIM):
            query = one_head(queries[span_of(b)], h)
            grad = one_head(grads[span_of(b)], h)
            scores = causal(nt(keys[:reach], query * BF16(FACTOR)))
            probs = jnp.exp(scores - sum_ref[0, h, :, span_of(b)])
            probs_grad = nt(values[:reach], grad)
            inner = jnp.sum(probs * probs_grad, axis=0, keepdims=True)
            score_grad = (probs * (probs_grad - inner)).astype(BF16)
            dv_part, dk_part = nn(probs.astype(BF16), grad), nn(score_grad, query)
            dv_sum = dv_part if dv_sum is None else dv_sum + dv_part
            dk_sum = dk_part if dk_sum is None else dk_sum + dk_part
            dq.append(nn(turned[head_of(h), :reach], score_grad))
        dq_heads.append(jnp.concatenate(dq, axis=0))
        dk.append(dk_sum)
        dv.append(dv_sum)

    def whole_rows(parts):
        early, late = parts
        return jnp.concatenate([late[:HALF_SEQ] + early, late[HALF_SEQ:]], axis=0)

    dq = jnp.concatenate(dq_heads, axis=1).T * FACTOR
    dk = whole_rows(dk) * FACTOR
    dv = whole_rows(dv).astype(BF16)
    copies = dq.shape[1] // PAIR
    cosine = jnp.concatenate([cos_ref[...]] * copies, axis=1)
    sine = jnp.concatenate([sin_ref[...]] * copies, axis=1)
    put_back(shift_ref, dq_ref, count, (dq * cosine - turn(dq) * sine).astype(BF16))
    put_back(shift_ref, dk_ref, count, (dk * cosine - turn(dk) * sine).astype(BF16))
    put_back(shift_ref, dv_ref, count, dv)


def attend_back(chain, shift, count, query, key, value, grad, logsum, tables):
    rows, width = query.shape
    grid, tile, sums = attention_specs(rows, width, PAIR)
    return chain.call(
        functools.partial(attend_back_body, count),
        grid,
        [tile] * 4 + [sums] + [whole((SEQ, PAIR))] * 2,
        [tile] * 3,
        [((rows, width), BF16)] * 3,
        flops=40 * rows * width * SEQ,
        prefetch=1,
        moved=14 * rows * width,
    )(shift, query, key, value, grad, logsum, *tables)


def local(
    chips,
    group,
    tokens,
    attn_gain,
    query_weight,
    key_weight,
    value_weight,
    output_weight,
    ffn_gain,
    gate_weight,
    up_weight,
    down_weight,
    cotangent,
):
    line = jnp.asarray(chips.table)[lax.axis_index("dp")]
    rows, model = tokens.shape
    count = SEQ // rows
    shift = lax.axis_index("tensor") % count
    row = jnp.arange(SEQ, dtype=jnp.int32)
    places = rope_tables(row)
    tables = rope_tables((row // rows ^ shift) * rows + row % rows)
    shift = jnp.reshape(shift, (1,)).astype(jnp.int32)
    early = (*places, *tables, line, shift)
    depth, own = query_weight.shape
    hidden_units = gate_weight.shape[1]
    chain = Chain()

    def gather(piece):
        return Gather(chips, chain, chain.join(piece)[0])

    def spread_of(values):
        return Spread(group, chain, chain.join(values)[0])

    def fold_of(part):
        own_part, sent = part
        sent = chain.join(*sent[0], *sent[1])
        return Fold(group, chain, own_part, [sent[: group.bits], sent[group.bits :]])

    def grads_of(left, rights, theirs=None):
        if theirs is None:
            (theirs,) = weight_grads(chain, left, 1, rights)
        got = [None]
        chain.ask(theirs, got, 0, chips.other)

        def mine(**how):
            if got[0] is None:
                chain.flush()
            blocks = weight_grads(chain, left, 0, rights, got[0], chips.bits)
            return Sums(chips, chain, blocks, **how)

        return mine

    extra = jnp.concatenate([attn_gain, ffn_gain, jnp.zeros((4 * own - 2 * depth,), BF16)])
    attn = jnp.concatenate([query_weight, key_weight, value_weight, output_weight.T], axis=1)
    attn = gather(jnp.concatenate([attn, jnp.broadcast_to(extra, (16, 4 * own))], axis=0))
    spread = spread_of(tokens)
    grads_spread = spread_of(cotangent)
    grads_spread.later = []
    down_turned, *early = chain.join(down_weight.T, *early)
    places, tables, line, shift = early[:2], early[2:4], early[4], early[5]
    chain.end(attn, spread, grads_spread)
    chain.end(attn, spread)
    all_tokens = spread.blocks()
    attn = attn.pieces()
    pair = gather(jnp.concatenate([gate_weight, up_weight], axis=1))
    w_query, w_key, w_value, w_output = [Weight(attn, depth, i * own, own) for i in range(4)]
    gains = jnp.concatenate(
        [piece[depth : depth + 1, : 2 * depth].reshape(2, depth) for piece in attn], axis=1
    ).astype(F32)

    group_one = ordered(chain, norm_body, line, gains, all_tokens)
    grads_spread.resume()
    query, key, value = project(chain, group_one, tables, w_query, w_key, w_value)
    mixed, logsum = attend(chain, shift, count, query, key, value)
    out_part = times_trans(chain, [(mixed, w_output)], group)
    fold = fold_of(out_part)
    chain.end(fold, pair, grads_spread)
    grad_rows = ordered(chain, order_body, line, gains, grads_spread.blocks())
    chain.end(fold)
    attended = fold.total()
    middle, second = by_rows(
        chain, middle_body, line, tokens, gains, attended, [], [F32, BF16]
    )
    spread = spread_of(second)
    chain.end(spread, pair)
    pair = pair.pieces()
    down = gather(down_turned)
    chain.end(spread)
    group_two = spread.blocks()
    w_gate = Weight(pair, depth, 0, hidden_units)
    w_up = Weight(pair, depth, hidden_units, hidden_units)
    hidden, slope, silu, theirs = gate_up(chain, group_two, w_gate, w_up, grad_rows)

    mine = grads_of(grad_rows, [hidden], theirs)
    chain.end(down)
    chain.flush()
    down_sum = mine()
    w_down = Weight(down.pieces(), depth, 0, hidden_units)
    gate_grad, up_grad, gate_theirs = hidden_back(
        chain, grad_rows, w_down, slope, silu, group_two
    )
    mine_gate = grads_of(group_two, [gate_grad], gate_theirs)
    chain.end(down_sum)
    second_part = times_trans(chain, [(gate_grad, w_gate), (up_grad, w_up)], group)
    fold = fold_of(second_part)
    gate_sum = mine_gate(hold=True)
    (up_theirs,) = weight_grads(chain, group_two, 1, [up_grad])
    chain.end(down_sum)
    mine_up = grads_of(group_two, [up_grad], up_theirs)
    chain.end(fold)
    up_sum = mine_up(hold=True)
    chain.end(fold)
    second_grad = fold.total()
    middle_grad, low_grad = by_rows(
        chain, second_back_body, line, cotangent, gains, second_grad, [middle], [F32, BF16]
    )
    spread = spread_of(low_grad)
    chain.end(gate_sum)
    gate_sum.resume()
    result_part = times_trans(chain, [(hidden, w_down)], group)
    chain.end(spread)
    (down_sum,) = finish(chain, down_sum.terms())
    chain.end(spread)
    attn_grads = spread.blocks()

    mixed_grad = mixed_back(chain, attn_grads, w_output)
    query_back, key_back, value_back = attend_back(
        chain, shift, count, query, key, value, mixed_grad, logsum, places
    )
    mine_qkv = grads_of(group_one, [query_back, key_back, value_back])
    mine_out = grads_of(attn_grads, [mixed])
    chain.end(gate_sum, up_sum)
    up_sum.resume()
    fold = fold_of(result_part)
    qkv_sum = mine_qkv()
    first_part = times_trans(
        chain, [(query_back, w_query), (key_back, w_key), (value_back, w_value)], group
    )
    out_sum = mine_out(hold=True)
    chain.end(fold)
    gate_sum, gate_inner = finish(chain, gate_sum.terms(), [gate_weight])
    chain.end(fold)
    result_part = fold.total()
    (layer_out,) = by_rows(chain, result_body, line, middle, gains, result_part, [], [BF16])
    fold = fold_of(first_part)
    chain.end(up_sum, out_sum)
    chain.end(qkv_sum)
    out_sum.resume()
    up_sum, up_inner = finish(chain, up_sum.terms(), [up_weight])
    chain.end(fold)
    chain.end(fold)
    first_grad = fold.total()
    (input_grad,) = by_rows(
        chain, first_back_body, line, tokens, gains, first_grad, [middle_grad], [F32]
    )
    chain.end(qkv_sum)
    query_sum, key_sum, value_sum, qkv_inner = finish(
        chain, qkv_sum.terms(), [query_weight, key_weight, value_weight]
    )
    gain_parts = jnp.stack(
        [qkv_inner / attn_gain.astype(F32), (gate_inner + up_inner) / ffn_gain.astype(F32)]
    )
    (gain_parts,) = chain.join(gain_parts)
    (out_sum,) = finish(chain, out_sum.terms())
    gain_totals = gain_parts
    for k in range(1, group.size):
        pairs = [(i, i ^ k) for i in range(group.size)]
        gain_totals += lax.ppermute(gain_parts, "tensor", pairs)
    gain_one_total, gain_two_total = gain_totals[0], gain_totals[1]
    return (
        layer_out,
        input_grad,
        gain_one_total,
        query_sum,
        key_sum,
        value_sum,
        out_sum,
        gain_two_total,
        gate_sum,
        up_sum,
        down_sum,
    )


def solution(mesh):
    in_specs = (
        P(("dp", "tensor"), None),
        P("dp"),
        P("dp", "tensor"),
        P("dp", "tensor"),
        P("dp", "tensor"),
        P("tensor", "dp"),
        P("dp"),
        P("dp", "tensor"),
        P("dp", "tensor"),
        P("tensor", "dp"),
        P(("dp", "tensor"), None),
    )
    out_specs = (
        P(("dp", "tensor"), None),
        P(("dp", "tensor"), None),
        P("dp"),
        P("dp", "tensor"),
        P("dp", "tensor"),
        P("dp", "tensor"),
        P("tensor", "dp"),
        P("dp"),
        P("dp", "tensor"),
        P("dp", "tensor"),
        P("tensor", "dp"),
    )
    chips = Chips(mesh.shape["dp"])
    size = mesh.shape["tensor"]
    links = [[(i, i ^ 1 << b) for i in range(size)] for b in range(size.bit_length() - 1)]
    group = Group(links, "tensor")

    def run(*arrays):
        return local(chips, group, *arrays)

    return jax.shard_map(run, mesh=mesh, in_specs=in_specs, out_specs=out_specs, check_vma=False)
```

profile of v0, /device:TPU:0, one launch (start us, length us, event | category | flops | bytes accessed | tf_op | source)
XLA Modules:
  0.0 620.4 jit_solution(7572850275927520798)
XLA Ops:
  12.9 18.1 %collective-permute-done.5.refs_4_ = bf16[256,2048]{1,0:T(8,128)(2,1)} collective-permute-done((bf16[256,2048]{1,0:T(8,128)(2,1)}, bf16[256,2048]{1,0:T(8,128)(2,1)}, u32[]{:S(2)}, u32[]{:S(2)}) %collective-permute-start.5) | collective-permute-done | bytes 1048608 | tf_op jit(solution)/shard_map/ppermute | solution.py:233
  41.1 11.6 %collective-permute-done.3.refs_4_ = bf16[256,2048]{1,0:T(8,128)(2,1)} collective-permute-done((bf16[256,2048]{1,0:T(8,128)(2,1)}, bf16[256,2048]{1,0:T(8,128)(2,1)}, u32[]{:S(2)}, u32[]{:S(2)}) %collective-permute-start.3) | collective-permute-done | bytes 1048608 | tf_op jit(solution)/shard_map/ppermute | solution.py:233
  68.8 6.8 %collective-permute-done.8.refs_6_ = bf16[256,1024]{1,0:T(8,128)(2,1)S(1)} collective-permute-done((bf16[256,1024]{1,0:T(8,128)(2,1)S(1)}, bf16[256,1024]{1,0:T(8,128)(2,1)S(1)}, u32[]{:S(2)}, u32[]{:S(2)}) %collective-permute-start.8) | collective-permute-done | bytes 524320 | tf_op jit(solution)/shard_map/ppermute | solution.py:233
  76.8 9.0 %collective-permute-done.6.refs_6_.refs_14_.refs_22_.refs_4_.refs_8_ = bf16[272,2048]{1,0:T(8,128)(2,1)S(1)} collective-permute-done((bf16[272,2048]{1,0:T(8,128)(2,1)S(1)}, bf16[272,2048]{1,0:T(8,128)(2,1)S(1)}, u32[]{:S(2)}, u32[]{:S(2)}) %collective-permute-start.6) | collective-permute-done | bytes 1114144 | tf_op jit(solution)/shard_map/ppermute | solution.py:111
  95.0 7.4 %shard_map.203 = (bf16[1024,2048]{1,0:T(8,128)(2,1)}, f32[8,128]{1,0:T(8,128)}) custom-call(s32[8]{0:T(128)} %dynamic-slice_bitcast_fusion.refs_0_, f32[2,2048]{1,0:T(2,128)} %convert_element_type.84.refs_1_.refs_2_, bf16[256,2048]{1,0:T(8,128)(2,1)} %refs_1_.5, bf16[256,2048]{1,0:T(8,128)(2,1)} %collective-permute-done.2.refs_3_, ...), custom_call_target="tpu_custom_call" | custom-call | flops 10240 | bytes 2048 | tf_op jit(solution)/shard_map/pallas_call | solution.py:89
  103.0 11.2 %shard_map.204 = (bf16[1024,512]{1,0:T(8,128)(2,1)}, bf16[1024,512]{1,0:T(8,128)(2,1)}, bf16[1024,512]{1,0:T(8,128)(2,1)}, f32[8,128]{1,0:T(8,128)}) custom-call(bf16[1024,2048]{1,0:T(8,128)(2,1)} %get-tuple-element.320.refs_0_, f32[512,128]{1,0:T(8,128)} %get-tuple-element.321.refs_1_, f32[512,128]{1,0:T(8,128)} %get-tuple-element.322.refs_2_, ...), custom_call_target="tpu_custom_call" | custom-call | flops 1572864 | bytes 3328 | tf_op jit(solution)/shard_map/pallas_call | solution.py:89
  114.2 11.4 %shard_map.205 = (bf16[1024,512]{1,0:T(8,128)(2,1)}, f32[2,8,1,512]{3,2,1,0:T(1,128)}, f32[8,128]{1,0:T(8,128)}) custom-call(s32[1]{0:T(128)} %bitcast.2.refs_0_, bf16[1024,512]{1,0:T(8,128)(2,1)} %get-tuple-element.327.refs_1_, bf16[1024,512]{1,0:T(8,128)(2,1)} %get-tuple-element.328.refs_2_, bf16[1024,512]{1,0:T(8,128)(2,1)} %get-tuple-element.329.refs_3_, ...), custom_call_target="tpu_custom_call" | custom-call | flops 1048576 | bytes 1024 | tf_op jit(solution)/shard_map/pallas_call | solution.py:89
  125.6 8.4 %shard_map.206 = (bf16[256,1024]{1,0:T(8,128)(2,1)}, bf16[256,1024]{1,0:T(8,128)(2,1)}, bf16[512,1024]{1,0:T(8,128)(2,1)}, bf16[256,1024]{1,0:T(8,128)(2,1)}, bf...) custom-call(bf16[1024,512]{1,0:T(8,128)(2,1)} %get-tuple-element.331.refs_0_.refs_4_, ...), custom_call_target="tpu_custom_call" | custom-call | flops 524288 | bytes 1792 | tf_op jit(solution)/shard_map/pallas_call | solution.py:89
  137.7 33.4 %collective-permute-done.18.refs_6_ = bf16[256,1024]{1,0:T(8,128)(2,1)S(1)} collective-permute-done((bf16[256,1024]{1,0:T(8,128)(2,1)S(1)}, bf16[256,1024]{1,0:T(8,128)(2,1)S(1)}, u32[]{:S(2)}, u32[]{:S(2)}) %collective-permute-start.18) | collective-permute-done | bytes 524320 | tf_op jit(solution)/shard_map/ppermute | solution.py:233
  171.1 9.1 %collective-permute-done.16.refs_7_.refs_15_.refs_4_.refs_12_ = bf16[256,4096]{1,0:T(8,128)(2,1)} collective-permute-done((bf16[256,4096]{1,0:T(8,128)(2,1)}, bf16[256,4096]{1,0:T(8,128)(2,1)}, u32[]{:S(2)}, u32[]{:S(2)}) %collective-permute-start.16) | collective-permute-done | bytes 2097184 | tf_op jit(solution)/shard_map/ppermute | solution.py:111
  187.2 6.3 %shard_map.208 = (bf16[1024,2048]{1,0:T(8,128)(2,1)}, f32[8,128]{1,0:T(8,128)}) custom-call(s32[8]{0:T(128)} %dynamic-slice_bitcast_fusion.refs_0_, f32[2,2048]{1,0:T(2,128)} %convert_element_type.84.refs_1_.refs_2_, bf16[256,2048]{1,0:T(8,128)(2,1)} %refs_1_.4, bf16[256,2048]{1,0:T(8,128)(2,1)} %collective-permute-done.4.refs_3_, ...), custom_call_target="tpu_custom_call" | custom-call | flops 10240 | bytes 2048 | tf_op jit(solution)/shard_map/pallas_call | solution.py:89
  206.2 27.7 %collective-permute-done.24.refs_8_.refs_16_.refs_5_.refs_13_ = bf16[256,4096]{1,0:T(8,128)(2,1)} collective-permute-done((bf16[256,4096]{1,0:T(8,128)(2,1)}, bf16[256,4096]{1,0:T(8,128)(2,1)}, u32[]{:S(2)}, u32[]{:S(2)}) %collective-permute-start.24) | collective-permute-done | bytes 2097184 | tf_op jit(solution)/shard_map/ppermute | solution.py:111
  239.2 9.3 %collective-permute-done.28.refs_4_.refs_14_.refs_3_ = bf16[256,1024]{1,0:T(8,128)(2,1)S(1)} collective-permute-done((bf16[256,1024]{1,0:T(8,128)(2,1)S(1)}, bf16[256,1024]{1,0:T(8,128)(2,1)S(1)}, u32[]{:S(2)}, u32[]{:S(2)}) %collective-permute-start.28) | collective-permute-done | bytes 524320 | tf_op jit(solution)/shard_map/ppermute | solution.py:233
  250.6 31.1 %shard_map.210 = (bf16[1024,2048]{1,0:T(8,128)(2,1)}, bf16[1024,2048]{1,0:T(8,128)(2,1)}, bf16[1024,2048]{1,0:T(8,128)(2,1)}, bf16[1024,2048]{1,0:T(8,128)(2,1)}, f32[8,128]{1,0:T(8,128)}) custom-call(bf16[256,2048]{1,0:T(8,128)(2,1)} %get-tuple-element.366.refs_0_.refs_11_, bf16[256,2048]{1,0:T(8,128)(2,1)} %copy-done.11, bf16[256,2048]{1,0:T(8,128)(2,1)} %copy-done.10, ...), custom_call_target="tpu_custom_call" | custom-call | flops 6291456 | bytes 8192 | tf_op jit(solution)/shard_map/pallas_call | solution.py:89
  285.9 9.6 %collective-permute-done.34.refs_2_ = bf16[1024,2048]{1,0:T(8,128)(2,1)} collective-permute-done((bf16[1024,2048]{1,0:T(8,128)(2,1)}, bf16[1024,2048]{1,0:T(8,128)(2,1)}, u32[]{:S(2)}, u32[]{:S(2)}) %collective-permute-start.34) | collective-permute-done | bytes 4194336 | tf_op jit(solution)/shard_map/ppermute | solution.py:114
  295.5 9.8 %shard_map.211 = (bf16[256,2048]{1,0:T(8,128)(2,1)}, bf16[256,2048]{1,0:T(8,128)(2,1)}, bf16[256,2048]{1,0:T(8,128)(2,1)}, bf16[256,2048]{1,0:T(8,128)(2,1)}, f32[8,128]{1,0:T(8,128)}) custom-call(bf16[1024,2048]{1,0:T(8,128)(2,1)} %get-tuple-element.382.refs_21_.refs_0_, bf16[1024,2048]{1,0:T(8,128)(2,1)} %get-tuple-element.384.refs_1_.refs_0_, ...), custom_call_target="tpu_custom_call" | custom-call | flops 1048576 | bytes 2560 | tf_op jit(solution)/shard_map/pallas_call | solution.py:89
  314.5 21.3 %shard_map.212 = (bf16[1024,2048]{1,0:T(8,128)(2,1)}, bf16[1024,2048]{1,0:T(8,128)(2,1)}, bf16[1024,2048]{1,0:T(8,128)(2,1)}, f32[8,128]{1,0:T(8,128)}) custom-call(bf16[1024,2048]{1,0:T(8,128)(2,1)} %get-tuple-element.382.refs_21_.refs_0_, bf16[256,2048]{1,0:T(8,128)(2,1)} %bitcast.refs_1_, bf16[256,2048]{1,0:T(8,128)(2,1)} %collective-permute-done.30.refs_2_, ...), custom_call_target="tpu_custom_call" | custom-call | flops 3145728 | bytes 7168 | tf_op jit(solution)/shard_map/pallas_call | solution.py:89
  341.3 23.3 %shard_map.213 = (bf16[256,1024]{1,0:T(8,128)(2,1)}, bf16[256,1024]{1,0:T(8,128)(2,1)}, bf16[512,1024]{1,0:T(8,128)(2,1)}, bf16[256,1024]{1,0:T(8,128)(2,1)}, bf...) custom-call(bf16[1024,2048]{1,0:T(8,128)(2,1)} %get-tuple-element.398.refs_0_.refs_4_, ...), custom_call_target="tpu_custom_call" | custom-call | flops 4194304 | bytes 7168 | tf_op jit(solution)/shard_map/pallas_call | solution.py:89
  366.7 10.1 %shard_map.214 = (bf16[256,2048]{1,0:T(8,128)(2,1)}, bf16[256,2048]{1,0:T(8,128)(2,1)}, bf16[256,2048]{1,0:T(8,128)(2,1)}, bf16[256,2048]{1,0:T(8,128)(2,1)}, f32[8,128]{1,0:T(8,128)}) custom-call(bf16[256,2048]{1,0:T(8,128)(2,1)} %get-tuple-element.366.refs_0_.refs_11_, bf16[256,2048]{1,0:T(8,128)(2,1)} %copy-done.11, bf16[256,2048]{1,0:T(8,128)(2,1)} %copy-done.10, ...), custom_call_target="tpu_custom_call" | custom-call | flops 1048576 | bytes 2560 | tf_op jit(solution)/shard_map/pallas_call | solution.py:89
  376.8 9.0 %shard_map.215 = (bf16[1024,2048]{1,0:T(8,128)(2,1)}, f32[8,128]{1,0:T(8,128)}) custom-call(bf16[256,2048]{1,0:T(8,128)(2,1)} %get-tuple-element.366.refs_0_.refs_11_, bf16[256,2048]{1,0:T(8,128)(2,1)} %copy-done.11, bf16[256,2048]{1,0:T(8,128)(2,1)} %copy-done.10, bf16[256,1024]{1,0:T(8,128)(2,1)} %copy-done.15, ...), custom_call_target="tpu_custom_call" | custom-call | flops 1048576 | bytes 2560 | tf_op jit(solution)/shard_map/pallas_call | solution.py:89
  397.6 9.8 %shard_map.217 = (bf16[256,2048]{1,0:T(8,128)(2,1)}, bf16[256,2048]{1,0:T(8,128)(2,1)}, bf16[256,2048]{1,0:T(8,128)(2,1)}, bf16[256,2048]{1,0:T(8,128)(2,1)}, f32[8,128]{1,0:T(8,128)}) custom-call(bf16[256,2048]{1,0:T(8,128)(2,1)} %get-tuple-element.366.refs_0_.refs_11_, bf16[256,2048]{1,0:T(8,128)(2,1)} %copy-done.11, bf16[256,2048]{1,0:T(8,128)(2,1)} %copy-done.10, ...), custom_call_target="tpu_custom_call" | custom-call | flops 1048576 | bytes 2560 | tf_op jit(solution)/shard_map/pallas_call | solution.py:89
  421.8 14.1 %shard_map.219 = (bf16[256,1024]{1,0:T(8,128)(2,1)}, bf16[256,1024]{1,0:T(8,128)(2,1)}, bf16[512,1024]{1,0:T(8,128)(2,1)}, bf16[256,1024]{1,0:T(8,128)(2,1)}, bf...) custom-call(bf16[1024,2048]{1,0:T(8,128)(2,1)} %get-tuple-element.384.refs_1_.refs_0_, ...), custom_call_target="tpu_custom_call" | custom-call | flops 2097152 | bytes 4096 | tf_op jit(solution)/shard_map/pallas_call | solution.py:89
  446.8 7.5 %collective-permute-done.54.refs_4_.refs_3_ = bf16[256,1024]{1,0:T(8,128)(2,1)S(1)} collective-permute-done((bf16[256,1024]{1,0:T(8,128)(2,1)}, bf16[256,1024]{1,0:T(8,128)(2,1)S(1)}, u32[]{:S(2)}, u32[]{:S(2)}) %collective-permute-start.54) | collective-permute-done | bytes 524320 | tf_op jit(solution)/shard_map/ppermute | solution.py:233
  456.4 6.9 %shard_map.221 = (bf16[1024,512]{1,0:T(8,128)(2,1)}, f32[8,128]{1,0:T(8,128)}) custom-call(bf16[256,2048]{1,0:T(8,128)(2,1)} %get-tuple-element.457.refs_0_, bf16[256,2048]{1,0:T(8,128)(2,1)} %copy-done.13, bf16[256,2048]{1,0:T(8,128)(2,1)} %copy-done.12, bf16[256,1024]{1,0:T(8,128)(2,1)} %copy-done.30, bf16[256,1024]{1,0:T(8,128)(2,1)} %copy-done.31, ...), custom_call_target="tpu_custom_call" | custom-call | flops 524288 | bytes 1792 | tf_op jit(solution)/shard_map/pallas_call | solution.py:89
  463.3 18.0 %shard_map.222 = (bf16[1024,512]{1,0:T(8,128)(2,1)}, bf16[1024,512]{1,0:T(8,128)(2,1)}, bf16[1024,512]{1,0:T(8,128)(2,1)}, f32[8,128]{1,0:T(8,128)}) custom-call(s32[1]{0:T(128)} %bitcast.2.refs_0_, bf16[1024,512]{1,0:T(8,128)(2,1)} %get-tuple-element.327.refs_1_, bf16[1024,512]{1,0:T(8,128)(2,1)} %get-tuple-element.328.refs_2_, ...), custom_call_target="tpu_custom_call" | custom-call | flops 2621440 | bytes 1792 | tf_op jit(solution)/shard_map/pallas_call | solution.py:89
  481.3 8.2 %shard_map.223 = (bf16[1024,1536]{1,0:T(8,128)(2,1)}, f32[8,128]{1,0:T(8,128)}) custom-call(bf16[1024,2048]{1,0:T(8,128)(2,1)} %get-tuple-element.320.refs_0_, bf16[1024,512]{1,0:T(8,128)(2,1)} %get-tuple-element.474.refs_1_.refs_0_, bf16[1024,512]{1,0:T(8,128)(2,1)} %get-tuple-element.475.refs_2_.refs_1_, ...), custom_call_target="tpu_custom_call" | custom-call | flops 786432 | bytes 2048 | tf_op jit(solution)/shard_map/pallas_call | solution.py:89
  502.6 8.7 %shard_map.225 = (bf16[256,1536]{1,0:T(8,128)(2,1)}, bf16[256,1536]{1,0:T(8,128)(2,1)}, bf16[256,1536]{1,0:T(8,128)(2,1)}, bf16[256,1536]{1,0:T(8,128)(2,1)}, f32[8,128]{1,0:T(8,128)}) custom-call(bf16[1024,2048]{1,0:T(8,128)(2,1)} %get-tuple-element.320.refs_0_, bf16[1024,512]{1,0:T(8,128)(2,1)} %get-tuple-element.474.refs_1_.refs_0_, ...), custom_call_target="tpu_custom_call" | custom-call | flops 786432 | bytes 2048 | tf_op jit(solution)/shard_map/pallas_call | solution.py:89
  511.3 12.1 %shard_map.226 = (bf16[256,1024]{1,0:T(8,128)(2,1)}, bf16[256,1024]{1,0:T(8,128)(2,1)}, bf16[512,1024]{1,0:T(8,128)(2,1)}, bf16[256,1024]{1,0:T(8,128)(2,1)}, bf...) custom-call(bf16[1024,512]{1,0:T(8,128)(2,1)} %get-tuple-element.474.refs_1_.refs_0_, ...), custom_call_target="tpu_custom_call" | custom-call | flops 1572864 | bytes 3328 | tf_op jit(solution)/shard_map/pallas_call | solution.py:89
  534.7 10.8 %collective-permute-done.59.refs_5_ = bf16[256,1024]{1,0:T(8,128)(2,1)S(1)} collective-permute-done((bf16[256,1024]{1,0:T(8,128)(2,1)}, bf16[256,1024]{1,0:T(8,128)(2,1)S(1)}, u32[]{:S(2)}, u32[]{:S(2)}) %collective-permute-start.59) | collective-permute-done | bytes 524320 | tf_op jit(solution)/shard_map/ppermute | solution.py:233
  556.5 12.6 %collective-permute-done.65 = bf16[256,512]{1,0:T(8,128)(2,1)S(1)} collective-permute-done((bf16[256,512]{1,0:T(8,128)(2,1)S(1)}, bf16[256,512]{1,0:T(8,128)(2,1)S(1)}, u32[]{:S(2)}, u32[]{:S(2)}) %collective-permute-start.65) | collective-permute-done | bytes 262176 | tf_op jit(solution)/shard_map/ppermute | solution.py:111
  586.2 9.0 %collective-permute-done.67.refs_5_ = bf16[256,1024]{1,0:T(8,128)(2,1)S(1)} collective-permute-done((bf16[256,1024]{1,0:T(8,128)(2,1)}, bf16[256,1024]{1,0:T(8,128)(2,1)S(1)}, u32[]{:S(2)}, u32[]{:S(2)}) %collective-permute-start.67) | collective-permute-done | bytes 524320 | tf_op jit(solution)/shard_map/ppermute | solution.py:233
  602.5 5.5 collective-permute-done.69.refs_1_
  (345 shorter events, 211.5 us)
Async XLA Ops:
  6.7 51.0 %collective-permute-start.1 = (bf16[272,2048]{1,0:T(8,128)(2,1)S(1)}, bf16[272,2048]{1,0:T(8,128)(2,1)S(1)}, u32[]{:S(2)}, u32[]{:S(2)}) collective-permute-start(bf16[272,2048]{1,0:T(8,128)(2,1)S(1)} %pad_maximum_fusion.1.refs_3_.refs_11_.refs_19_.refs_1_.refs_5_), channel_id=1, source_target_pairs={{0,8},{4,12},{8,0},{12,4},{16,24},{20,28},{24,16},{28,20},{1,9},{5... | collective-permute-start | bytes 3342344 | tf_op jit(solution)/shard_map/ppermute | solution.py:111
  8.3 50.6 %collective-permute-start = (bf16[272,2048]{1,0:T(8,128)(2,1)S(1)}, bf16[272,2048]{1,0:T(8,128)(2,1)S(1)}, u32[]{:S(2)}, u32[]{:S(2)}) collective-permute-start(bf16[272,2048]{1,0:T(8,128)(2,1)S(1)} %pad_maximum_fusion.1.refs_3_.refs_11_.refs_19_.refs_1_.refs_5_), channel_id=1, source_target_pairs={{0,16},{4,20},{8,24},{12,28},{16,0},{20,4},{24,8},{28,12},{1,17},{... | collective-permute-start | bytes 3342344 | tf_op jit(solution)/shard_map/ppermute | solution.py:111
  10.9 30.2 %collective-permute-start.4 = (bf16[256,2048]{1,0:T(8,128)(2,1)}, bf16[256,2048]{1,0:T(8,128)(2,1)}, u32[]{:S(2)}, u32[]{:S(2)}) collective-permute-start(bf16[256,2048]{1,0:T(8,128)(2,1)} %refs_1_.4), channel_id=1, source_target_pairs={{0,1},{1,0},{2,3},{3,2},{4,5},{5,4},{6,7},{7,6},{8,9},{9,8},{10,11... | collective-permute-start | bytes 3145736 | tf_op jit(solution)/shard_map/ppermute | solution.py:233
  12.4 40.3 %collective-permute-start.3 = (bf16[256,2048]{1,0:T(8,128)(2,1)}, bf16[256,2048]{1,0:T(8,128)(2,1)}, u32[]{:S(2)}, u32[]{:S(2)}) collective-permute-start(bf16[256,2048]{1,0:T(8,128)(2,1)} %refs_1_.5), channel_id=1, source_target_pairs={{0,2},{1,3},{2,0},{3,1},{4,6},{5,7},{6,4},{7,5},{8,10},{9,11},{10,... | collective-permute-start | bytes 3145736 | tf_op jit(solution)/shard_map/ppermute | solution.py:233
  87.6 92.6 %collective-permute-start.16 = (bf16[256,4096]{1,0:T(8,128)(2,1)}, bf16[256,4096]{1,0:T(8,128)(2,1)}, u32[]{:S(2)}, u32[]{:S(2)}) collective-permute-start(bf16[256,4096]{1,0:T(8,128)(2,1)} %pad_maximum_fusion.refs_5_.refs_13_.refs_2_.refs_10_), channel_id=1, source_target_pairs={{0,8},{4,12},{8,0},{12,4},{16,24},{20,28},{24,16},{28,20},{1,9},{5... | collective-permute-start | bytes 6291464 | tf_op jit(solution)/shard_map/ppermute | solution.py:111
  88.1 93.6 %collective-permute-start.15 = (bf16[256,4096]{1,0:T(8,128)(2,1)}, bf16[256,4096]{1,0:T(8,128)(2,1)}, u32[]{:S(2)}, u32[]{:S(2)}) collective-permute-start(bf16[256,4096]{1,0:T(8,128)(2,1)} %pad_maximum_fusion.refs_5_.refs_13_.refs_2_.refs_10_), channel_id=1, source_target_pairs={{0,16},{4,20},{8,24},{12,28},{16,0},{20,4},{24,8},{28,12},{1,17},{... | collective-permute-start | bytes 6291464 | tf_op jit(solution)/shard_map/ppermute | solution.py:111
  102.4 34.7 %collective-permute-start.17 = (bf16[256,1024]{1,0:T(8,128)(2,1)S(1)}, bf16[256,1024]{1,0:T(8,128)(2,1)S(1)}, u32[]{:S(2)}, u32[]{:S(2)}) collective-permute-start(bf16[256,1024]{1,0:T(8,128)(2,1)S(1)} %copy-done.55), channel_id=1, source_target_pairs={{0,2},{1,3},{2,0},{3,1},{4,6},{5,7},{6,4},{7,5},{8,10},{9,11},{10,... | collective-permute-start | bytes 1572872 | tf_op jit(solution)/shard_map/ppermute | solution.py:233
  134.0 47.6 %collective-permute-start.13 = (bf16[512,1024]{1,0:T(8,128)(2,1)}, bf16[512,1024]{1,0:T(8,128)(2,1)S(1)}, u32[]{:S(2)}, u32[]{:S(2)}) collective-permute-start(bf16[512,1024]{1,0:T(8,128)(2,1)} %get-tuple-element.339), channel_id=1, source_target_pairs={{0,2},{1,3},{2,0},{3,1},{4,6},{5,7},{6,4},{7,5},{8,10},{9,11},{10,... | collective-permute-start | bytes 3145736 | tf_op jit(solution)/shard_map/ppermute | solution.py:233
  135.6 46.1 %collective-permute-start.14 = (bf16[512,1024]{1,0:T(8,128)(2,1)}, bf16[512,1024]{1,0:T(8,128)(2,1)}, u32[]{:S(2)}, u32[]{:S(2)}) collective-permute-start(bf16[512,1024]{1,0:T(8,128)(2,1)} %get-tuple-element.340), channel_id=1, source_target_pairs={{0,1},{1,0},{2,3},{3,2},{4,5},{5,4},{6,7},{7,6},{8,9},{9,8},{10,11... | collective-permute-start | bytes 3145736 | tf_op jit(solution)/shard_map/ppermute | solution.py:233
  137.1 34.0 %collective-permute-start.18 = (bf16[256,1024]{1,0:T(8,128)(2,1)S(1)}, bf16[256,1024]{1,0:T(8,128)(2,1)S(1)}, u32[]{:S(2)}, u32[]{:S(2)}) collective-permute-start(bf16[256,1024]{1,0:T(8,128)(2,1)S(1)} %copy-done.54), channel_id=1, source_target_pairs={{0,1},{1,0},{2,3},{3,2},{4,5},{5,4},{6,7},{7,6},{8,9},{9,8},{10,11... | collective-permute-start | bytes 1572872 | tf_op jit(solution)/shard_map/ppermute | solution.py:233
  187.0 46.9 %collective-permute-start.24 = (bf16[256,4096]{1,0:T(8,128)(2,1)}, bf16[256,4096]{1,0:T(8,128)(2,1)}, u32[]{:S(2)}, u32[]{:S(2)}) collective-permute-start(bf16[256,4096]{1,0:T(8,128)(2,1)} %collective-permute-done.15.refs_6_.refs_14_.refs_3_.refs_11_), channel_id=1, source_target_pairs={{0,8},{4,12},{8,0},{12,4},{16,24},{20,28},{24,16},{28,20},{1,9},{5... | collective-permute-start | bytes 6291464 | tf_op jit(solution)/shard_map/ppermute | solution.py:111
  199.9 34.1 %collective-permute-start.25 = (bf16[256,4096]{1,0:T(8,128)(2,1)}, bf16[256,4096]{1,0:T(8,128)(2,1)S(1)}, u32[]{:S(2)}, u32[]{:S(2)}) collective-permute-start(bf16[256,4096]{1,0:T(8,128)(2,1)} %collective-permute-done.15.refs_6_.refs_14_.refs_3_.refs_11_), channel_id=1, source_target_pairs={{0,4},{4,0},{8,12},{12,8},{16,20},{20,16},{24,28},{28,24},{1,5},{5... | collective-permute-start | bytes 6291464 | tf_op jit(solution)/shard_map/ppermute | solution.py:114
  200.0 34.0 %collective-permute-start.26 = (bf16[256,4096]{1,0:T(8,128)(2,1)}, bf16[256,4096]{1,0:T(8,128)(2,1)}, u32[]{:S(2)}, u32[]{:S(2)}) collective-permute-start(bf16[256,4096]{1,0:T(8,128)(2,1)} %collective-permute-done.16.refs_7_.refs_15_.refs_4_.refs_12_), channel_id=1, source_target_pairs={{0,4},{4,0},{8,12},{12,8},{16,20},{20,16},{24,28},{28,24},{1,5},{5... | collective-permute-start | bytes 6291464 | tf_op jit(solution)/shard_map/ppermute | solution.py:114
  205.1 28.8 %collective-permute-start.23 = (bf16[256,2048]{1,0:T(8,128)(2,1)}, bf16[256,2048]{1,0:T(8,128)(2,1)S(1)}, u32[]{:S(2)}, u32[]{:S(2)}) collective-permute-start(bf16[256,2048]{1,0:T(8,128)(2,1)} %get-tuple-element.366.refs_0_.refs_11_), channel_id=1, source_target_pairs={{0,2},{1,3},{2,0},{3,1},{4,6},{5,7},{6,4},{7,5},{8,10},{9,11},{10,... | collective-permute-start | bytes 3145736 | tf_op jit(solution)/shard_map/ppermute | solution.py:233
  205.7 28.2 %collective-permute-start.22 = (bf16[256,2048]{1,0:T(8,128)(2,1)}, bf16[256,2048]{1,0:T(8,128)(2,1)S(1)}, u32[]{:S(2)}, u32[]{:S(2)}) collective-permute-start(bf16[256,2048]{1,0:T(8,128)(2,1)} %get-tuple-element.366.refs_0_.refs_11_), channel_id=1, source_target_pairs={{0,1},{1,0},{2,3},{3,2},{4,5},{5,4},{6,7},{7,6},{8,9},{9,8},{10,11... | collective-permute-start | bytes 3145736 | tf_op jit(solution)/shard_map/ppermute | solution.py:233
  236.3 47.5 %collective-permute-start.31 = (bf16[256,2048]{1,0:T(8,128)(2,1)}, bf16[256,2048]{1,0:T(8,128)(2,1)}, u32[]{:S(2)}, u32[]{:S(2)}) collective-permute-start(bf16[256,2048]{1,0:T(8,128)(2,1)} %bitcast.refs_1_), channel_id=1, source_target_pairs={{0,8},{4,12},{8,0},{12,4},{16,24},{20,28},{24,16},{28,20},{1,9},{5... | collective-permute-start | bytes 3145736 | tf_op jit(solution)/shard_map/ppermute | solution.py:111
  236.5 48.5 %collective-permute-start.30 = (bf16[256,2048]{1,0:T(8,128)(2,1)}, bf16[256,2048]{1,0:T(8,128)(2,1)}, u32[]{:S(2)}, u32[]{:S(2)}) collective-permute-start(bf16[256,2048]{1,0:T(8,128)(2,1)} %bitcast.refs_1_), channel_id=1, source_target_pairs={{0,16},{4,20},{8,24},{12,28},{16,0},{20,4},{24,8},{28,12},{1,17},{... | collective-permute-start | bytes 3145736 | tf_op jit(solution)/shard_map/ppermute | solution.py:111
  248.8 36.3 %collective-permute-start.32 = (bf16[256,2048]{1,0:T(8,128)(2,1)}, bf16[256,2048]{1,0:T(8,128)(2,1)}, u32[]{:S(2)}, u32[]{:S(2)}) collective-permute-start(bf16[256,2048]{1,0:T(8,128)(2,1)} %bitcast.refs_1_), channel_id=1, source_target_pairs={{0,4},{4,0},{8,12},{12,8},{16,20},{20,16},{24,28},{28,24},{1,5},{5... | collective-permute-start | bytes 3145736 | tf_op jit(solution)/shard_map/ppermute | solution.py:114
  336.7 29.9 %collective-permute-start.39 = (bf16[1024,2048]{1,0:T(8,128)(2,1)}, bf16[1024,2048]{1,0:T(8,128)(2,1)}, u32[]{:S(2)}, u32[]{:S(2)}) collective-permute-start(bf16[1024,2048]{1,0:T(8,128)(2,1)} %get-tuple-element.402), channel_id=1, source_target_pairs={{0,4},{4,0},{8,12},{12,8},{16,20},{20,16},{24,28},{28,24},{1,5},{5... | collective-permute-start | bytes 12582920 | tf_op jit(solution)/shard_map/ppermute | solution.py:114
  338.3 48.2 %collective-permute-start.43 = (bf16[256,2048]{1,0:T(8,128)(2,1)}, bf16[256,2048]{1,0:T(8,128)(2,1)S(1)}, u32[]{:S(2)}, u32[]{:S(2)}) collective-permute-start(bf16[256,2048]{1,0:T(8,128)(2,1)} %get-tuple-element.423), channel_id=1, source_target_pairs={{0,8},{4,12},{8,0},{12,4},{16,24},{20,28},{24,16},{28,20},{1,9},{5... | collective-permute-start | bytes 3145736 | tf_op jit(solution)/shard_map/ppermute | solution.py:111
  338.7 48.8 %collective-permute-start.44 = (bf16[256,2048]{1,0:T(8,128)(2,1)S(1)}, bf16[256,2048]{1,0:T(8,128)(2,1)S(1)}, u32[]{:S(2)}, u32[]{:S(2)}) collective-permute-start(bf16[256,2048]{1,0:T(8,128)(2,1)S(1)} %add_convert_fusion.2), channel_id=1, source_target_pairs={{0,16},{4,20},{8,24},{12,28},{16,0},{20,4},{24,8},{28,12},{1,17},{... | collective-permute-start | bytes 3145736 | tf_op jit(solution)/shard_map/ppermute | solution.py:111
  418.3 75.4 %collective-permute-start.48 = (bf16[256,2048]{1,0:T(8,128)(2,1)}, bf16[256,2048]{1,0:T(8,128)(2,1)S(1)}, u32[]{:S(2)}, u32[]{:S(2)}) collective-permute-start(bf16[256,2048]{1,0:T(8,128)(2,1)} %get-tuple-element.454), channel_id=1, source_target_pairs={{0,8},{4,12},{8,0},{12,4},{16,24},{20,28},{24,16},{28,20},{1,9},{5... | collective-permute-start | bytes 3145736 | tf_op jit(solution)/shard_map/ppermute | solution.py:111
  419.7 74.0 %collective-permute-start.49 = (bf16[256,2048]{1,0:T(8,128)(2,1)}, bf16[256,2048]{1,0:T(8,128)(2,1)S(1)}, u32[]{:S(2)}, u32[]{:S(2)}) collective-permute-start(bf16[256,2048]{1,0:T(8,128)(2,1)} %add_convert_fusion.1), channel_id=1, source_target_pairs={{0,16},{4,20},{8,24},{12,28},{16,0},{20,4},{24,8},{28,12},{1,17},{... | collective-permute-start | bytes 3145736 | tf_op jit(solution)/shard_map/ppermute | solution.py:111
  420.3 73.4 %collective-permute-start.50 = (bf16[256,2048]{1,0:T(8,128)(2,1)}, bf16[256,2048]{1,0:T(8,128)(2,1)}, u32[]{:S(2)}, u32[]{:S(2)}) collective-permute-start(bf16[256,2048]{1,0:T(8,128)(2,1)} %get-tuple-element.456), channel_id=1, source_target_pairs={{0,8},{4,12},{8,0},{12,4},{16,24},{20,28},{24,16},{28,20},{1,9},{5... | collective-permute-start | bytes 3145736 | tf_op jit(solution)/shard_map/ppermute | solution.py:111
  498.2 29.5 %collective-permute-start.55 = (bf16[512,1024]{1,0:T(8,128)(2,1)}, bf16[512,1024]{1,0:T(8,128)(2,1)S(1)}, u32[]{:S(2)}, u32[]{:S(2)}) collective-permute-start(bf16[512,1024]{1,0:T(8,128)(2,1)} %get-tuple-element.485), channel_id=1, source_target_pairs={{0,2},{1,3},{2,0},{3,1},{4,6},{5,7},{6,4},{7,5},{8,10},{9,11},{10,... | collective-permute-start | bytes 3145736 | tf_op jit(solution)/shard_map/ppermute | solution.py:233
  498.8 28.9 %collective-permute-start.56 = (bf16[512,1024]{1,0:T(8,128)(2,1)}, bf16[512,1024]{1,0:T(8,128)(2,1)S(1)}, u32[]{:S(2)}, u32[]{:S(2)}) collective-permute-start(bf16[512,1024]{1,0:T(8,128)(2,1)} %get-tuple-element.486), channel_id=1, source_target_pairs={{0,1},{1,0},{2,3},{3,2},{4,5},{5,4},{6,7},{7,6},{8,9},{9,8},{10,11... | collective-permute-start | bytes 3145736 | tf_op jit(solution)/shard_map/ppermute | solution.py:233
  499.4 55.7 %collective-permute-start.63 = (bf16[256,2048]{1,0:T(8,128)(2,1)}, bf16[256,2048]{1,0:T(8,128)(2,1)}, u32[]{:S(2)}, u32[]{:S(2)}) collective-permute-start(bf16[256,2048]{1,0:T(8,128)(2,1)} %get-tuple-element.519), channel_id=1, source_target_pairs={{0,8},{4,12},{8,0},{12,4},{16,24},{20,28},{24,16},{28,20},{1,9},{5... | collective-permute-start | bytes 3145736 | tf_op jit(solution)/shard_map/ppermute | solution.py:111
  500.9 55.6 %collective-permute-start.64 = (bf16[256,2048]{1,0:T(8,128)(2,1)}, bf16[256,2048]{1,0:T(8,128)(2,1)}, u32[]{:S(2)}, u32[]{:S(2)}) collective-permute-start(bf16[256,2048]{1,0:T(8,128)(2,1)} %add_convert_fusion), channel_id=1, source_target_pairs={{0,16},{4,20},{8,24},{12,28},{16,0},{20,4},{24,8},{28,12},{1,17},{... | collective-permute-start | bytes 3145736 | tf_op jit(solution)/shard_map/ppermute | solution.py:111
  532.0 37.1 %collective-permute-start.66 = (bf16[256,1536]{1,0:T(8,128)(2,1)S(1)}, bf16[256,1536]{1,0:T(8,128)(2,1)S(1)}, u32[]{:S(2)}, u32[]{:S(2)}) collective-permute-start(bf16[256,1536]{1,0:T(8,128)(2,1)S(1)} %copy-done.64), channel_id=1, source_target_pairs={{0,8},{4,12},{8,0},{12,4},{16,24},{20,28},{24,16},{28,20},{1,9},{5... | collective-permute-start | bytes 2359304 | tf_op jit(solution)/shard_map/ppermute | solution.py:111
  569.3 38.8 %collective-permute-start.69 = (bf16[256,1536]{1,0:T(8,128)(2,1)}, bf16[256,1536]{1,0:T(8,128)(2,1)S(1)}, u32[]{:S(2)}, u32[]{:S(2)}) collective-permute-start(bf16[256,1536]{1,0:T(8,128)(2,1)} %get-tuple-element.552), channel_id=1, source_target_pairs={{0,8},{4,12},{8,0},{12,4},{16,24},{20,28},{24,16},{28,20},{1,9},{5... | collective-permute-start | bytes 2359304 | tf_op jit(solution)/shard_map/ppermute | solution.py:111
  569.7 38.4 %collective-permute-start.70 = (bf16[256,1536]{1,0:T(8,128)(2,1)S(1)}, bf16[256,1536]{1,0:T(8,128)(2,1)S(1)}, u32[]{:S(2)}, u32[]{:S(2)}) collective-permute-start(bf16[256,1536]{1,0:T(8,128)(2,1)S(1)} %add_convert_fusion.3), channel_id=1, source_target_pairs={{0,16},{4,20},{8,24},{12,28},{16,0},{20,4},{24,8},{28,12},{1,17},{... | collective-permute-start | bytes 2359304 | tf_op jit(solution)/shard_map/ppermute | solution.py:111
  584.5 32.2 %collective-permute-start.74 = (bf16[256,512]{1,0:T(8,128)(2,1)}, bf16[256,512]{1,0:T(8,128)(2,1)S(1)}, u32[]{:S(2)}, u32[]{:S(2)}) collective-permute-start(bf16[256,512]{1,0:T(8,128)(2,1)} %get-tuple-element.567), channel_id=1, source_target_pairs={{0,8},{4,12},{8,0},{12,4},{16,24},{20,28},{24,16},{28,20},{1,9},{5... | collective-permute-start | bytes 786440 | tf_op jit(solution)/shard_map/ppermute | solution.py:111
  (110 other events, 1367.1 us)
where the time goes:
time: 631 us; the launch traced here: 620 us
  Pallas kernels  280 us (44%)
  waiting for transfers between devices  226 us (36%)
  starting transfers between devices  66.4 us (11%)
  local copies, waits for them, and re-layouts  32.5 us (5%)
  other arithmetic  14.6 us (2%)
    pallas_call x33, Pallas kernels, with_token(): *results, self.token = run(*args, self.token)  280 us
    ppermute x32, waiting for transfers between devices, send(): return lax.ppermute(value, self.axes, self.links[bit])  133 us
    ppermute x24, waiting for transfers between devices, send(): return lax.ppermute(value, 'dp', self.links[p])  77.9 us
    ppermute x32, starting transfers between devices, send(): return lax.ppermute(value, self.axes, self.links[bit])  35.4 us
    ppermute x24, starting transfers between devices, send(): return lax.ppermute(value, 'dp', self.links[p])  25.1 us
    unnamed x141, local copies, waits for them, and re-layouts  19.1 us
    ppermute x17, waiting for transfers between devices, other(): return lax.ppermute(value, 'dp', self.swap)  14.7 us
  transfers between devices with their start and end apart: 76, of which 38 were waited for; matrix products, arithmetic and copies ran while one was open for 4% of the time, Pallas kernels for 45%

commit v1 on v0

--- a/solution.py
+++ b/solution.py
@@ -761,24 +761,32 @@
 def mixed_back_body(n, counts, *refs):
     m = sum(counts)
     out_ref, x_ref, sems = refs[m + n :]
-
-    @pl.when(pl.program_id(0) == 0)
-    def _():
-        collect(counts, refs, x_ref, sems)
-
-    out_ref[...] = nn(x_ref[...], joined(refs[m : m + n])).astype(BF16)
+    rows = x_ref.shape[0] // len(counts)
+    blocks, i = [], 0
+    for k, count in enumerate(counts):
+        half = x_ref.shape[1] // count
+        blocks.append([])
+        for h in range(count):
+            target = x_ref.at[pl.ds(k * rows, rows), pl.ds(h * half, half)]
+            blocks[-1].append(pltpu.make_async_copy(refs[i], target, sems.at[i]))
+            blocks[-1][-1].start()
+            i += 1
+    weight = joined(refs[m : m + n])
+    for k, copies in enumerate(blocks):
+        for copy in copies:
+            copy.wait()
+        out_ref[cut(rows, k), :] = nn(x_ref[cut(rows, k), :], weight).astype(BF16)
 
 
 def mixed_back(chain, held, out):
     counts, arrays, specs, scratch = collected(held)
     rows, model = scratch[0].shape
     n, width = len(out.pieces), out.width
-    tile = min(256, width)
     return chain.call(
         functools.partial(mixed_back_body, n, counts),
-        (width // tile,),
-        specs + out.tiles(tile),
-        [pl.BlockSpec((rows, tile), lambda j: (0, j))],
+        (1,),
+        specs + out.tiles(width),
+        [whole((rows, width))],
         [((rows, width), BF16)],
         flops=2 * rows * model * width,
         scratch=scratch,

time: 631 us -> 631 us (level)
  transfers between devices with their start and end apart: 76 -> 76, of which waited for: 38 -> 39; matrix products, arithmetic and copies ran while one was open for 4% -> 4% of each run, Pallas kernels for 45% -> 45%
where the time goes in v1:
time: 631 us; the launch traced here: 620 us
  Pallas kernels  280 us (44%)
  waiting for transfers between devices  226 us (36%)
  starting transfers between devices  66.7 us (11%)
  local copies, waits for them, and re-layouts  32.5 us (5%)
  other arithmetic  14.6 us (2%)
    pallas_call x33, Pallas kernels, with_token(): *results, self.token = run(*args, self.token)  280 us
    ppermute x32, waiting for transfers between devices, send(): return lax.ppermute(value, self.axes, self.links[bit])  133 us
    ppermute x24, waiting for transfers between devices, send(): return lax.ppermute(value, 'dp', self.links[p])  77.9 us
    ppermute x32, starting transfers between devices, send(): return lax.ppermute(value, self.axes, self.links[bit])  35.4 us
    ppermute x24, starting transfers between devices, send(): return lax.ppermute(value, 'dp', self.links[p])  25.5 us
    unnamed x141, local copies, waits for them, and re-layouts  19 us
    ppermute x17, waiting for transfers between devices, other(): return lax.ppermute(value, 'dp', self.swap)  14.7 us
  transfers between devices with their start and end apart: 76, of which 39 were waited for; matrix products, arithmetic and copies ran while one was open for 4% of the time, Pallas kernels for 45%

profile of v1, /device:TPU:0, one launch (start us, length us, event | category | flops | bytes accessed | tf_op | source)
XLA Modules:
  0.0 620.5 jit_solution(1308253877344163877)
XLA Ops:
  12.9 18.1 %collective-permute-done.5.refs_4_ = bf16[256,2048]{1,0:T(8,128)(2,1)} collective-permute-done((bf16[256,2048]{1,0:T(8,128)(2,1)}, bf16[256,2048]{1,0:T(8,128)(2,1)}, u32[]{:S(2)}, u32[]{:S(2)}) %collective-permute-start.5) | collective-permute-done | bytes 1048608 | tf_op jit(solution)/shard_map/ppermute | solution.py:233
  41.1 11.6 %collective-permute-done.3.refs_4_ = bf16[256,2048]{1,0:T(8,128)(2,1)} collective-permute-done((bf16[256,2048]{1,0:T(8,128)(2,1)}, bf16[256,2048]{1,0:T(8,128)(2,1)}, u32[]{:S(2)}, u32[]{:S(2)}) %collective-permute-start.3) | collective-permute-done | bytes 1048608 | tf_op jit(solution)/shard_map/ppermute | solution.py:233
  68.8 6.8 %collective-permute-done.8.refs_6_ = bf16[256,1024]{1,0:T(8,128)(2,1)S(1)} collective-permute-done((bf16[256,1024]{1,0:T(8,128)(2,1)S(1)}, bf16[256,1024]{1,0:T(8,128)(2,1)S(1)}, u32[]{:S(2)}, u32[]{:S(2)}) %collective-permute-start.8) | collective-permute-done | bytes 524320 | tf_op jit(solution)/shard_map/ppermute | solution.py:233
  76.8 9.0 %collective-permute-done.6.refs_6_.refs_14_.refs_22_.refs_4_.refs_8_ = bf16[272,2048]{1,0:T(8,128)(2,1)S(1)} collective-permute-done((bf16[272,2048]{1,0:T(8,128)(2,1)S(1)}, bf16[272,2048]{1,0:T(8,128)(2,1)S(1)}, u32[]{:S(2)}, u32[]{:S(2)}) %collective-permute-start.6) | collective-permute-done | bytes 1114144 | tf_op jit(solution)/shard_map/ppermute | solution.py:111
  95.0 7.4 %shard_map.203 = (bf16[1024,2048]{1,0:T(8,128)(2,1)}, f32[8,128]{1,0:T(8,128)}) custom-call(s32[8]{0:T(128)} %dynamic-slice_bitcast_fusion.refs_0_, f32[2,2048]{1,0:T(2,128)} %convert_element_type.84.refs_1_.refs_2_, bf16[256,2048]{1,0:T(8,128)(2,1)} %refs_1_.5, bf16[256,2048]{1,0:T(8,128)(2,1)} %collective-permute-done.2.refs_3_, ...), custom_call_target="tpu_custom_call" | custom-call | flops 10240 | bytes 2048 | tf_op jit(solution)/shard_map/pallas_call | solution.py:89
  103.0 11.2 %shard_map.204 = (bf16[1024,512]{1,0:T(8,128)(2,1)}, bf16[1024,512]{1,0:T(8,128)(2,1)}, bf16[1024,512]{1,0:T(8,128)(2,1)}, f32[8,128]{1,0:T(8,128)}) custom-call(bf16[1024,2048]{1,0:T(8,128)(2,1)} %get-tuple-element.320.refs_0_, f32[512,128]{1,0:T(8,128)} %get-tuple-element.321.refs_1_, f32[512,128]{1,0:T(8,128)} %get-tuple-element.322.refs_2_, ...), custom_call_target="tpu_custom_call" | custom-call | flops 1572864 | bytes 3328 | tf_op jit(solution)/shard_map/pallas_call | solution.py:89
  114.1 11.4 %shard_map.205 = (bf16[1024,512]{1,0:T(8,128)(2,1)}, f32[2,8,1,512]{3,2,1,0:T(1,128)}, f32[8,128]{1,0:T(8,128)}) custom-call(s32[1]{0:T(128)} %bitcast.2.refs_0_, bf16[1024,512]{1,0:T(8,128)(2,1)} %get-tuple-element.327.refs_1_, bf16[1024,512]{1,0:T(8,128)(2,1)} %get-tuple-element.328.refs_2_, bf16[1024,512]{1,0:T(8,128)(2,1)} %get-tuple-element.329.refs_3_, ...), custom_call_target="tpu_custom_call" | custom-call | flops 1048576 | bytes 1024 | tf_op jit(solution)/shard_map/pallas_call | solution.py:89
  125.6 8.4 %shard_map.206 = (bf16[256,1024]{1,0:T(8,128)(2,1)}, bf16[256,1024]{1,0:T(8,128)(2,1)}, bf16[512,1024]{1,0:T(8,128)(2,1)}, bf16[256,1024]{1,0:T(8,128)(2,1)}, bf...) custom-call(bf16[1024,512]{1,0:T(8,128)(2,1)} %get-tuple-element.331.refs_0_.refs_4_, ...), custom_call_target="tpu_custom_call" | custom-call | flops 524288 | bytes 1792 | tf_op jit(solution)/shard_map/pallas_call | solution.py:89
  137.7 33.4 %collective-permute-done.18.refs_6_ = bf16[256,1024]{1,0:T(8,128)(2,1)S(1)} collective-permute-done((bf16[256,1024]{1,0:T(8,128)(2,1)S(1)}, bf16[256,1024]{1,0:T(8,128)(2,1)S(1)}, u32[]{:S(2)}, u32[]{:S(2)}) %collective-permute-start.18) | collective-permute-done | bytes 524320 | tf_op jit(solution)/shard_map/ppermute | solution.py:233
  171.1 9.2 %collective-permute-done.16.refs_7_.refs_15_.refs_4_.refs_12_ = bf16[256,4096]{1,0:T(8,128)(2,1)} collective-permute-done((bf16[256,4096]{1,0:T(8,128)(2,1)}, bf16[256,4096]{1,0:T(8,128)(2,1)}, u32[]{:S(2)}, u32[]{:S(2)}) %collective-permute-start.16) | collective-permute-done | bytes 2097184 | tf_op jit(solution)/shard_map/ppermute | solution.py:111
  187.2 6.3 %shard_map.208 = (bf16[1024,2048]{1,0:T(8,128)(2,1)}, f32[8,128]{1,0:T(8,128)}) custom-call(s32[8]{0:T(128)} %dynamic-slice_bitcast_fusion.refs_0_, f32[2,2048]{1,0:T(2,128)} %convert_element_type.84.refs_1_.refs_2_, bf16[256,2048]{1,0:T(8,128)(2,1)} %refs_1_.4, bf16[256,2048]{1,0:T(8,128)(2,1)} %collective-permute-done.4.refs_3_, ...), custom_call_target="tpu_custom_call" | custom-call | flops 10240 | bytes 2048 | tf_op jit(solution)/shard_map/pallas_call | solution.py:89
  206.4 27.5 %collective-permute-done.24.refs_8_.refs_16_.refs_5_.refs_13_ = bf16[256,4096]{1,0:T(8,128)(2,1)} collective-permute-done((bf16[256,4096]{1,0:T(8,128)(2,1)}, bf16[256,4096]{1,0:T(8,128)(2,1)}, u32[]{:S(2)}, u32[]{:S(2)}) %collective-permute-start.24) | collective-permute-done | bytes 2097184 | tf_op jit(solution)/shard_map/ppermute | solution.py:111
  239.2 9.3 %collective-permute-done.28.refs_4_.refs_14_.refs_3_ = bf16[256,1024]{1,0:T(8,128)(2,1)S(1)} collective-permute-done((bf16[256,1024]{1,0:T(8,128)(2,1)S(1)}, bf16[256,1024]{1,0:T(8,128)(2,1)S(1)}, u32[]{:S(2)}, u32[]{:S(2)}) %collective-permute-start.28) | collective-permute-done | bytes 524320 | tf_op jit(solution)/shard_map/ppermute | solution.py:233
  250.6 31.1 %shard_map.210 = (bf16[1024,2048]{1,0:T(8,128)(2,1)}, bf16[1024,2048]{1,0:T(8,128)(2,1)}, bf16[1024,2048]{1,0:T(8,128)(2,1)}, bf16[1024,2048]{1,0:T(8,128)(2,1)}, f32[8,128]{1,0:T(8,128)}) custom-call(bf16[256,2048]{1,0:T(8,128)(2,1)} %get-tuple-element.366.refs_0_.refs_11_, bf16[256,2048]{1,0:T(8,128)(2,1)} %copy-done.11, bf16[256,2048]{1,0:T(8,128)(2,1)} %copy-done.10, ...), custom_call_target="tpu_custom_call" | custom-call | flops 6291456 | bytes 8192 | tf_op jit(solution)/shard_map/pallas_call | solution.py:89
  285.9 9.6 %collective-permute-done.34.refs_2_ = bf16[1024,2048]{1,0:T(8,128)(2,1)} collective-permute-done((bf16[1024,2048]{1,0:T(8,128)(2,1)}, bf16[1024,2048]{1,0:T(8,128)(2,1)}, u32[]{:S(2)}, u32[]{:S(2)}) %collective-permute-start.34) | collective-permute-done | bytes 4194336 | tf_op jit(solution)/shard_map/ppermute | solution.py:114
  295.5 9.8 %shard_map.211 = (bf16[256,2048]{1,0:T(8,128)(2,1)}, bf16[256,2048]{1,0:T(8,128)(2,1)}, bf16[256,2048]{1,0:T(8,128)(2,1)}, bf16[256,2048]{1,0:T(8,128)(2,1)}, f32[8,128]{1,0:T(8,128)}) custom-call(bf16[1024,2048]{1,0:T(8,128)(2,1)} %get-tuple-element.382.refs_21_.refs_0_, bf16[1024,2048]{1,0:T(8,128)(2,1)} %get-tuple-element.384.refs_1_.refs_0_, ...), custom_call_target="tpu_custom_call" | custom-call | flops 1048576 | bytes 2560 | tf_op jit(solution)/shard_map/pallas_call | solution.py:89
  305.3 5.5 collective-permute-done.33.refs_4_
  314.5 21.3 %shard_map.212 = (bf16[1024,2048]{1,0:T(8,128)(2,1)}, bf16[1024,2048]{1,0:T(8,128)(2,1)}, bf16[1024,2048]{1,0:T(8,128)(2,1)}, f32[8,128]{1,0:T(8,128)}) custom-call(bf16[1024,2048]{1,0:T(8,128)(2,1)} %get-tuple-element.382.refs_21_.refs_0_, bf16[256,2048]{1,0:T(8,128)(2,1)} %bitcast.refs_1_, bf16[256,2048]{1,0:T(8,128)(2,1)} %collective-permute-done.30.refs_2_, ...), custom_call_target="tpu_custom_call" | custom-call | flops 3145728 | bytes 7168 | tf_op jit(solution)/shard_map/pallas_call | solution.py:89
  341.3 23.3 %shard_map.213 = (bf16[256,1024]{1,0:T(8,128)(2,1)}, bf16[256,1024]{1,0:T(8,128)(2,1)}, bf16[512,1024]{1,0:T(8,128)(2,1)}, bf16[256,1024]{1,0:T(8,128)(2,1)}, bf...) custom-call(bf16[1024,2048]{1,0:T(8,128)(2,1)} %get-tuple-element.398.refs_0_.refs_4_, ...), custom_call_target="tpu_custom_call" | custom-call | flops 4194304 | bytes 7168 | tf_op jit(solution)/shard_map/pallas_call | solution.py:89
  366.7 9.9 %shard_map.214 = (bf16[256,2048]{1,0:T(8,128)(2,1)}, bf16[256,2048]{1,0:T(8,128)(2,1)}, bf16[256,2048]{1,0:T(8,128)(2,1)}, bf16[256,2048]{1,0:T(8,128)(2,1)}, f32[8,128]{1,0:T(8,128)}) custom-call(bf16[256,2048]{1,0:T(8,128)(2,1)} %get-tuple-element.366.refs_0_.refs_11_, bf16[256,2048]{1,0:T(8,128)(2,1)} %copy-done.11, bf16[256,2048]{1,0:T(8,128)(2,1)} %copy-done.10, ...), custom_call_target="tpu_custom_call" | custom-call | flops 1048576 | bytes 2560 | tf_op jit(solution)/shard_map/pallas_call | solution.py:89
  376.5 9.0 %shard_map.215 = (bf16[1024,2048]{1,0:T(8,128)(2,1)}, f32[8,128]{1,0:T(8,128)}) custom-call(bf16[256,2048]{1,0:T(8,128)(2,1)} %get-tuple-element.366.refs_0_.refs_11_, bf16[256,2048]{1,0:T(8,128)(2,1)} %copy-done.11, bf16[256,2048]{1,0:T(8,128)(2,1)} %copy-done.10, bf16[256,1024]{1,0:T(8,128)(2,1)} %copy-done.15, ...), custom_call_target="tpu_custom_call" | custom-call | flops 1048576 | bytes 2560 | tf_op jit(solution)/shard_map/pallas_call | solution.py:89
  397.6 9.8 %shard_map.217 = (bf16[256,2048]{1,0:T(8,128)(2,1)}, bf16[256,2048]{1,0:T(8,128)(2,1)}, bf16[256,2048]{1,0:T(8,128)(2,1)}, bf16[256,2048]{1,0:T(8,128)(2,1)}, f32[8,128]{1,0:T(8,128)}) custom-call(bf16[256,2048]{1,0:T(8,128)(2,1)} %get-tuple-element.366.refs_0_.refs_11_, bf16[256,2048]{1,0:T(8,128)(2,1)} %copy-done.11, bf16[256,2048]{1,0:T(8,128)(2,1)} %copy-done.10, ...), custom_call_target="tpu_custom_call" | custom-call | flops 1048576 | bytes 2560 | tf_op jit(solution)/shard_map/pallas_call | solution.py:89
  421.8 14.1 %shard_map.219 = (bf16[256,1024]{1,0:T(8,128)(2,1)}, bf16[256,1024]{1,0:T(8,128)(2,1)}, bf16[512,1024]{1,0:T(8,128)(2,1)}, bf16[256,1024]{1,0:T(8,128)(2,1)}, bf...) custom-call(bf16[1024,2048]{1,0:T(8,128)(2,1)} %get-tuple-element.384.refs_1_.refs_0_, ...), custom_call_target="tpu_custom_call" | custom-call | flops 2097152 | bytes 4096 | tf_op jit(solution)/shard_map/pallas_call | solution.py:89
  446.8 7.5 %collective-permute-done.54.refs_4_.refs_3_ = bf16[256,1024]{1,0:T(8,128)(2,1)S(1)} collective-permute-done((bf16[256,1024]{1,0:T(8,128)(2,1)}, bf16[256,1024]{1,0:T(8,128)(2,1)S(1)}, u32[]{:S(2)}, u32[]{:S(2)}) %collective-permute-start.54) | collective-permute-done | bytes 524320 | tf_op jit(solution)/shard_map/ppermute | solution.py:233
  456.4 6.7 %shard_map.221 = (bf16[1024,512]{1,0:T(8,128)(2,1)}, f32[8,128]{1,0:T(8,128)}) custom-call(bf16[256,2048]{1,0:T(8,128)(2,1)} %get-tuple-element.457.refs_0_, bf16[256,2048]{1,0:T(8,128)(2,1)} %copy-done.13, bf16[256,2048]{1,0:T(8,128)(2,1)} %copy-done.12, bf16[256,1024]{1,0:T(8,128)(2,1)} %copy-done.30, bf16[256,1024]{1,0:T(8,128)(2,1)} %copy-done.31, ...), custom_call_target="tpu_custom_call" | custom-call | flops 524288 | bytes 1792 | tf_op jit(solution)/shard_map/pallas_call | solution.py:89
  463.1 17.9 %shard_map.222 = (bf16[1024,512]{1,0:T(8,128)(2,1)}, bf16[1024,512]{1,0:T(8,128)(2,1)}, bf16[1024,512]{1,0:T(8,128)(2,1)}, f32[8,128]{1,0:T(8,128)}) custom-call(s32[1]{0:T(128)} %bitcast.2.refs_0_, bf16[1024,512]{1,0:T(8,128)(2,1)} %get-tuple-element.327.refs_1_, bf16[1024,512]{1,0:T(8,128)(2,1)} %get-tuple-element.328.refs_2_, ...), custom_call_target="tpu_custom_call" | custom-call | flops 2621440 | bytes 1792 | tf_op jit(solution)/shard_map/pallas_call | solution.py:89
  481.0 8.3 %shard_map.223 = (bf16[1024,1536]{1,0:T(8,128)(2,1)}, f32[8,128]{1,0:T(8,128)}) custom-call(bf16[1024,2048]{1,0:T(8,128)(2,1)} %get-tuple-element.320.refs_0_, bf16[1024,512]{1,0:T(8,128)(2,1)} %get-tuple-element.474.refs_1_.refs_0_, bf16[1024,512]{1,0:T(8,128)(2,1)} %get-tuple-element.475.refs_2_.refs_1_, ...), custom_call_target="tpu_custom_call" | custom-call | flops 786432 | bytes 2048 | tf_op jit(solution)/shard_map/pallas_call | solution.py:89
  502.4 8.7 %shard_map.225 = (bf16[256,1536]{1,0:T(8,128)(2,1)}, bf16[256,1536]{1,0:T(8,128)(2,1)}, bf16[256,1536]{1,0:T(8,128)(2,1)}, bf16[256,1536]{1,0:T(8,128)(2,1)}, f32[8,128]{1,0:T(8,128)}) custom-call(bf16[1024,2048]{1,0:T(8,128)(2,1)} %get-tuple-element.320.refs_0_, bf16[1024,512]{1,0:T(8,128)(2,1)} %get-tuple-element.474.refs_1_.refs_0_, ...), custom_call_target="tpu_custom_call" | custom-call | flops 786432 | bytes 2048 | tf_op jit(solution)/shard_map/pallas_call | solution.py:89
  511.1 12.1 %shard_map.226 = (bf16[256,1024]{1,0:T(8,128)(2,1)}, bf16[256,1024]{1,0:T(8,128)(2,1)}, bf16[512,1024]{1,0:T(8,128)(2,1)}, bf16[256,1024]{1,0:T(8,128)(2,1)}, bf...) custom-call(bf16[1024,512]{1,0:T(8,128)(2,1)} %get-tuple-element.474.refs_1_.refs_0_, ...), custom_call_target="tpu_custom_call" | custom-call | flops 1572864 | bytes 3328 | tf_op jit(solution)/shard_map/pallas_call | solution.py:89
  534.5 10.8 %collective-permute-done.59.refs_5_ = bf16[256,1024]{1,0:T(8,128)(2,1)S(1)} collective-permute-done((bf16[256,1024]{1,0:T(8,128)(2,1)}, bf16[256,1024]{1,0:T(8,128)(2,1)S(1)}, u32[]{:S(2)}, u32[]{:S(2)}) %collective-permute-start.59) | collective-permute-done | bytes 524320 | tf_op jit(solution)/shard_map/ppermute | solution.py:233
  556.2 12.6 %collective-permute-done.65 = bf16[256,512]{1,0:T(8,128)(2,1)S(1)} collective-permute-done((bf16[256,512]{1,0:T(8,128)(2,1)S(1)}, bf16[256,512]{1,0:T(8,128)(2,1)S(1)}, u32[]{:S(2)}, u32[]{:S(2)}) %collective-permute-start.65) | collective-permute-done | bytes 262176 | tf_op jit(solution)/shard_map/ppermute | solution.py:111
  586.0 9.0 %collective-permute-done.67.refs_5_ = bf16[256,1024]{1,0:T(8,128)(2,1)S(1)} collective-permute-done((bf16[256,1024]{1,0:T(8,128)(2,1)}, bf16[256,1024]{1,0:T(8,128)(2,1)S(1)}, u32[]{:S(2)}, u32[]{:S(2)}) %collective-permute-start.67) | collective-permute-done | bytes 524320 | tf_op jit(solution)/shard_map/ppermute | solution.py:233
  (345 shorter events, 212.0 us)
Async XLA Ops:
  6.7 51.0 %collective-permute-start.1 = (bf16[272,2048]{1,0:T(8,128)(2,1)S(1)}, bf16[272,2048]{1,0:T(8,128)(2,1)S(1)}, u32[]{:S(2)}, u32[]{:S(2)}) collective-permute-start(bf16[272,2048]{1,0:T(8,128)(2,1)S(1)} %pad_maximum_fusion.1.refs_3_.refs_11_.refs_19_.refs_1_.refs_5_), channel_id=1, source_target_pairs={{0,8},{4,12},{8,0},{12,4},{16,24},{20,28},{24,16},{28,20},{1,9},{5... | collective-permute-start | bytes 3342344 | tf_op jit(solution)/shard_map/ppermute | solution.py:111
  8.3 50.6 %collective-permute-start = (bf16[272,2048]{1,0:T(8,128)(2,1)S(1)}, bf16[272,2048]{1,0:T(8,128)(2,1)S(1)}, u32[]{:S(2)}, u32[]{:S(2)}) collective-permute-start(bf16[272,2048]{1,0:T(8,128)(2,1)S(1)} %pad_maximum_fusion.1.refs_3_.refs_11_.refs_19_.refs_1_.refs_5_), channel_id=1, source_target_pairs={{0,16},{4,20},{8,24},{12,28},{16,0},{20,4},{24,8},{28,12},{1,17},{... | collective-permute-start | bytes 3342344 | tf_op jit(solution)/shard_map/ppermute | solution.py:111
  10.9 30.2 %collective-permute-start.4 = (bf16[256,2048]{1,0:T(8,128)(2,1)}, bf16[256,2048]{1,0:T(8,128)(2,1)}, u32[]{:S(2)}, u32[]{:S(2)}) collective-permute-start(bf16[256,2048]{1,0:T(8,128)(2,1)} %refs_1_.4), channel_id=1, source_target_pairs={{0,1},{1,0},{2,3},{3,2},{4,5},{5,4},{6,7},{7,6},{8,9},{9,8},{10,11... | collective-permute-start | bytes 3145736 | tf_op jit(solution)/shard_map/ppermute | solution.py:233
  12.4 40.3 %collective-permute-start.3 = (bf16[256,2048]{1,0:T(8,128)(2,1)}, bf16[256,2048]{1,0:T(8,128)(2,1)}, u32[]{:S(2)}, u32[]{:S(2)}) collective-permute-start(bf16[256,2048]{1,0:T(8,128)(2,1)} %refs_1_.5), channel_id=1, source_target_pairs={{0,2},{1,3},{2,0},{3,1},{4,6},{5,7},{6,4},{7,5},{8,10},{9,11},{10,... | collective-permute-start | bytes 3145736 | tf_op jit(solution)/shard_map/ppermute | solution.py:233
  87.6 92.6 %collective-permute-start.16 = (bf16[256,4096]{1,0:T(8,128)(2,1)}, bf16[256,4096]{1,0:T(8,128)(2,1)}, u32[]{:S(2)}, u32[]{:S(2)}) collective-permute-start(bf16[256,4096]{1,0:T(8,128)(2,1)} %pad_maximum_fusion.refs_5_.refs_13_.refs_2_.refs_10_), channel_id=1, source_target_pairs={{0,8},{4,12},{8,0},{12,4},{16,24},{20,28},{24,16},{28,20},{1,9},{5... | collective-permute-start | bytes 6291464 | tf_op jit(solution)/shard_map/ppermute | solution.py:111
  88.1 93.6 %collective-permute-start.15 = (bf16[256,4096]{1,0:T(8,128)(2,1)}, bf16[256,4096]{1,0:T(8,128)(2,1)}, u32[]{:S(2)}, u32[]{:S(2)}) collective-permute-start(bf16[256,4096]{1,0:T(8,128)(2,1)} %pad_maximum_fusion.refs_5_.refs_13_.refs_2_.refs_10_), channel_id=1, source_target_pairs={{0,16},{4,20},{8,24},{12,28},{16,0},{20,4},{24,8},{28,12},{1,17},{... | collective-permute-start | bytes 6291464 | tf_op jit(solution)/shard_map/ppermute | solution.py:111
  102.4 34.7 %collective-permute-start.17 = (bf16[256,1024]{1,0:T(8,128)(2,1)S(1)}, bf16[256,1024]{1,0:T(8,128)(2,1)S(1)}, u32[]{:S(2)}, u32[]{:S(2)}) collective-permute-start(bf16[256,1024]{1,0:T(8,128)(2,1)S(1)} %copy-done.55), channel_id=1, source_target_pairs={{0,2},{1,3},{2,0},{3,1},{4,6},{5,7},{6,4},{7,5},{8,10},{9,11},{10,... | collective-permute-start | bytes 1572872 | tf_op jit(solution)/shard_map/ppermute | solution.py:233
  134.0 47.6 %collective-permute-start.13 = (bf16[512,1024]{1,0:T(8,128)(2,1)}, bf16[512,1024]{1,0:T(8,128)(2,1)S(1)}, u32[]{:S(2)}, u32[]{:S(2)}) collective-permute-start(bf16[512,1024]{1,0:T(8,128)(2,1)} %get-tuple-element.339), channel_id=1, source_target_pairs={{0,2},{1,3},{2,0},{3,1},{4,6},{5,7},{6,4},{7,5},{8,10},{9,11},{10,... | collective-permute-start | bytes 3145736 | tf_op jit(solution)/shard_map/ppermute | solution.py:233
  135.6 46.1 %collective-permute-start.14 = (bf16[512,1024]{1,0:T(8,128)(2,1)}, bf16[512,1024]{1,0:T(8,128)(2,1)}, u32[]{:S(2)}, u32[]{:S(2)}) collective-permute-start(bf16[512,1024]{1,0:T(8,128)(2,1)} %get-tuple-element.340), channel_id=1, source_target_pairs={{0,1},{1,0},{2,3},{3,2},{4,5},{5,4},{6,7},{7,6},{8,9},{9,8},{10,11... | collective-permute-start | bytes 3145736 | tf_op jit(solution)/shard_map/ppermute | solution.py:233
  137.1 34.0 %collective-permute-start.18 = (bf16[256,1024]{1,0:T(8,128)(2,1)S(1)}, bf16[256,1024]{1,0:T(8,128)(2,1)S(1)}, u32[]{:S(2)}, u32[]{:S(2)}) collective-permute-start(bf16[256,1024]{1,0:T(8,128)(2,1)S(1)} %copy-done.54), channel_id=1, source_target_pairs={{0,1},{1,0},{2,3},{3,2},{4,5},{5,4},{6,7},{7,6},{8,9},{9,8},{10,11... | collective-permute-start | bytes 1572872 | tf_op jit(solution)/shard_map/ppermute | solution.py:233
  187.0 46.9 %collective-permute-start.24 = (bf16[256,4096]{1,0:T(8,128)(2,1)}, bf16[256,4096]{1,0:T(8,128)(2,1)}, u32[]{:S(2)}, u32[]{:S(2)}) collective-permute-start(bf16[256,4096]{1,0:T(8,128)(2,1)} %collective-permute-done.15.refs_6_.refs_14_.refs_3_.refs_11_), channel_id=1, source_target_pairs={{0,8},{4,12},{8,0},{12,4},{16,24},{20,28},{24,16},{28,20},{1,9},{5... | collective-permute-start | bytes 6291464 | tf_op jit(solution)/shard_map/ppermute | solution.py:111
  199.9 34.1 %collective-permute-start.25 = (bf16[256,4096]{1,0:T(8,128)(2,1)}, bf16[256,4096]{1,0:T(8,128)(2,1)S(1)}, u32[]{:S(2)}, u32[]{:S(2)}) collective-permute-start(bf16[256,4096]{1,0:T(8,128)(2,1)} %collective-permute-done.15.refs_6_.refs_14_.refs_3_.refs_11_), channel_id=1, source_target_pairs={{0,4},{4,0},{8,12},{12,8},{16,20},{20,16},{24,28},{28,24},{1,5},{5... | collective-permute-start | bytes 6291464 | tf_op jit(solution)/shard_map/ppermute | solution.py:114
  200.0 34.0 %collective-permute-start.26 = (bf16[256,4096]{1,0:T(8,128)(2,1)}, bf16[256,4096]{1,0:T(8,128)(2,1)}, u32[]{:S(2)}, u32[]{:S(2)}) collective-permute-start(bf16[256,4096]{1,0:T(8,128)(2,1)} %collective-permute-done.16.refs_7_.refs_15_.refs_4_.refs_12_), channel_id=1, source_target_pairs={{0,4},{4,0},{8,12},{12,8},{16,20},{20,16},{24,28},{28,24},{1,5},{5... | collective-permute-start | bytes 6291464 | tf_op jit(solution)/shard_map/ppermute | solution.py:114
  205.3 28.6 %collective-permute-start.23 = (bf16[256,2048]{1,0:T(8,128)(2,1)}, bf16[256,2048]{1,0:T(8,128)(2,1)S(1)}, u32[]{:S(2)}, u32[]{:S(2)}) collective-permute-start(bf16[256,2048]{1,0:T(8,128)(2,1)} %get-tuple-element.366.refs_0_.refs_11_), channel_id=1, source_target_pairs={{0,2},{1,3},{2,0},{3,1},{4,6},{5,7},{6,4},{7,5},{8,10},{9,11},{10,... | collective-permute-start | bytes 3145736 | tf_op jit(solution)/shard_map/ppermute | solution.py:233
  205.9 28.0 %collective-permute-start.22 = (bf16[256,2048]{1,0:T(8,128)(2,1)}, bf16[256,2048]{1,0:T(8,128)(2,1)S(1)}, u32[]{:S(2)}, u32[]{:S(2)}) collective-permute-start(bf16[256,2048]{1,0:T(8,128)(2,1)} %get-tuple-element.366.refs_0_.refs_11_), channel_id=1, source_target_pairs={{0,1},{1,0},{2,3},{3,2},{4,5},{5,4},{6,7},{7,6},{8,9},{9,8},{10,11... | collective-permute-start | bytes 3145736 | tf_op jit(solution)/shard_map/ppermute | solution.py:233
  236.3 47.5 %collective-permute-start.31 = (bf16[256,2048]{1,0:T(8,128)(2,1)}, bf16[256,2048]{1,0:T(8,128)(2,1)}, u32[]{:S(2)}, u32[]{:S(2)}) collective-permute-start(bf16[256,2048]{1,0:T(8,128)(2,1)} %bitcast.refs_1_), channel_id=1, source_target_pairs={{0,8},{4,12},{8,0},{12,4},{16,24},{20,28},{24,16},{28,20},{1,9},{5... | collective-permute-start | bytes 3145736 | tf_op jit(solution)/shard_map/ppermute | solution.py:111
  236.5 48.5 %collective-permute-start.30 = (bf16[256,2048]{1,0:T(8,128)(2,1)}, bf16[256,2048]{1,0:T(8,128)(2,1)}, u32[]{:S(2)}, u32[]{:S(2)}) collective-permute-start(bf16[256,2048]{1,0:T(8,128)(2,1)} %bitcast.refs_1_), channel_id=1, source_target_pairs={{0,16},{4,20},{8,24},{12,28},{16,0},{20,4},{24,8},{28,12},{1,17},{... | collective-permute-start | bytes 3145736 | tf_op jit(solution)/shard_map/ppermute | solution.py:111
  248.8 36.3 %collective-permute-start.32 = (bf16[256,2048]{1,0:T(8,128)(2,1)}, bf16[256,2048]{1,0:T(8,128)(2,1)}, u32[]{:S(2)}, u32[]{:S(2)}) collective-permute-start(bf16[256,2048]{1,0:T(8,128)(2,1)} %bitcast.refs_1_), channel_id=1, source_target_pairs={{0,4},{4,0},{8,12},{12,8},{16,20},{20,16},{24,28},{28,24},{1,5},{5... | collective-permute-start | bytes 3145736 | tf_op jit(solution)/shard_map/ppermute | solution.py:114
  336.7 29.9 %collective-permute-start.39 = (bf16[1024,2048]{1,0:T(8,128)(2,1)}, bf16[1024,2048]{1,0:T(8,128)(2,1)}, u32[]{:S(2)}, u32[]{:S(2)}) collective-permute-start(bf16[1024,2048]{1,0:T(8,128)(2,1)} %get-tuple-element.402), channel_id=1, source_target_pairs={{0,4},{4,0},{8,12},{12,8},{16,20},{20,16},{24,28},{28,24},{1,5},{5... | collective-permute-start | bytes 12582920 | tf_op jit(solution)/shard_map/ppermute | solution.py:114
  338.3 48.2 %collective-permute-start.43 = (bf16[256,2048]{1,0:T(8,128)(2,1)}, bf16[256,2048]{1,0:T(8,128)(2,1)S(1)}, u32[]{:S(2)}, u32[]{:S(2)}) collective-permute-start(bf16[256,2048]{1,0:T(8,128)(2,1)} %get-tuple-element.423), channel_id=1, source_target_pairs={{0,8},{4,12},{8,0},{12,4},{16,24},{20,28},{24,16},{28,20},{1,9},{5... | collective-permute-start | bytes 3145736 | tf_op jit(solution)/shard_map/ppermute | solution.py:111
  338.7 48.8 %collective-permute-start.44 = (bf16[256,2048]{1,0:T(8,128)(2,1)S(1)}, bf16[256,2048]{1,0:T(8,128)(2,1)S(1)}, u32[]{:S(2)}, u32[]{:S(2)}) collective-permute-start(bf16[256,2048]{1,0:T(8,128)(2,1)S(1)} %add_convert_fusion.2), channel_id=1, source_target_pairs={{0,16},{4,20},{8,24},{12,28},{16,0},{20,4},{24,8},{28,12},{1,17},{... | collective-permute-start | bytes 3145736 | tf_op jit(solution)/shard_map/ppermute | solution.py:111
  418.3 75.2 %collective-permute-start.48 = (bf16[256,2048]{1,0:T(8,128)(2,1)}, bf16[256,2048]{1,0:T(8,128)(2,1)S(1)}, u32[]{:S(2)}, u32[]{:S(2)}) collective-permute-start(bf16[256,2048]{1,0:T(8,128)(2,1)} %get-tuple-element.454), channel_id=1, source_target_pairs={{0,8},{4,12},{8,0},{12,4},{16,24},{20,28},{24,16},{28,20},{1,9},{5... | collective-permute-start | bytes 3145736 | tf_op jit(solution)/shard_map/ppermute | solution.py:111
  419.7 73.8 %collective-permute-start.49 = (bf16[256,2048]{1,0:T(8,128)(2,1)}, bf16[256,2048]{1,0:T(8,128)(2,1)S(1)}, u32[]{:S(2)}, u32[]{:S(2)}) collective-permute-start(bf16[256,2048]{1,0:T(8,128)(2,1)} %add_convert_fusion.1), channel_id=1, source_target_pairs={{0,16},{4,20},{8,24},{12,28},{16,0},{20,4},{24,8},{28,12},{1,17},{... | collective-permute-start | bytes 3145736 | tf_op jit(solution)/shard_map/ppermute | solution.py:111
  420.3 73.2 %collective-permute-start.50 = (bf16[256,2048]{1,0:T(8,128)(2,1)}, bf16[256,2048]{1,0:T(8,128)(2,1)}, u32[]{:S(2)}, u32[]{:S(2)}) collective-permute-start(bf16[256,2048]{1,0:T(8,128)(2,1)} %get-tuple-element.456), channel_id=1, source_target_pairs={{0,8},{4,12},{8,0},{12,4},{16,24},{20,28},{24,16},{28,20},{1,9},{5... | collective-permute-start | bytes 3145736 | tf_op jit(solution)/shard_map/ppermute | solution.py:111
  497.9 29.5 %collective-permute-start.55 = (bf16[512,1024]{1,0:T(8,128)(2,1)}, bf16[512,1024]{1,0:T(8,128)(2,1)S(1)}, u32[]{:S(2)}, u32[]{:S(2)}) collective-permute-start(bf16[512,1024]{1,0:T(8,128)(2,1)} %get-tuple-element.485), channel_id=1, source_target_pairs={{0,2},{1,3},{2,0},{3,1},{4,6},{5,7},{6,4},{7,5},{8,10},{9,11},{10,... | collective-permute-start | bytes 3145736 | tf_op jit(solution)/shard_map/ppermute | solution.py:233
  498.5 28.9 %collective-permute-start.56 = (bf16[512,1024]{1,0:T(8,128)(2,1)}, bf16[512,1024]{1,0:T(8,128)(2,1)S(1)}, u32[]{:S(2)}, u32[]{:S(2)}) collective-permute-start(bf16[512,1024]{1,0:T(8,128)(2,1)} %get-tuple-element.486), channel_id=1, source_target_pairs={{0,1},{1,0},{2,3},{3,2},{4,5},{5,4},{6,7},{7,6},{8,9},{9,8},{10,11... | collective-permute-start | bytes 3145736 | tf_op jit(solution)/shard_map/ppermute | solution.py:233
  499.2 55.7 %collective-permute-start.63 = (bf16[256,2048]{1,0:T(8,128)(2,1)}, bf16[256,2048]{1,0:T(8,128)(2,1)}, u32[]{:S(2)}, u32[]{:S(2)}) collective-permute-start(bf16[256,2048]{1,0:T(8,128)(2,1)} %get-tuple-element.519), channel_id=1, source_target_pairs={{0,8},{4,12},{8,0},{12,4},{16,24},{20,28},{24,16},{28,20},{1,9},{5... | collective-permute-start | bytes 3145736 | tf_op jit(solution)/shard_map/ppermute | solution.py:111
  500.7 55.6 %collective-permute-start.64 = (bf16[256,2048]{1,0:T(8,128)(2,1)}, bf16[256,2048]{1,0:T(8,128)(2,1)}, u32[]{:S(2)}, u32[]{:S(2)}) collective-permute-start(bf16[256,2048]{1,0:T(8,128)(2,1)} %add_convert_fusion), channel_id=1, source_target_pairs={{0,16},{4,20},{8,24},{12,28},{16,0},{20,4},{24,8},{28,12},{1,17},{... | collective-permute-start | bytes 3145736 | tf_op jit(solution)/shard_map/ppermute | solution.py:111
  531.8 37.1 %collective-permute-start.66 = (bf16[256,1536]{1,0:T(8,128)(2,1)S(1)}, bf16[256,1536]{1,0:T(8,128)(2,1)S(1)}, u32[]{:S(2)}, u32[]{:S(2)}) collective-permute-start(bf16[256,1536]{1,0:T(8,128)(2,1)S(1)} %copy-done.64), channel_id=1, source_target_pairs={{0,8},{4,12},{8,0},{12,4},{16,24},{20,28},{24,16},{28,20},{1,9},{5... | collective-permute-start | bytes 2359304 | tf_op jit(solution)/shard_map/ppermute | solution.py:111
  569.1 38.9 %collective-permute-start.69 = (bf16[256,1536]{1,0:T(8,128)(2,1)}, bf16[256,1536]{1,0:T(8,128)(2,1)S(1)}, u32[]{:S(2)}, u32[]{:S(2)}) collective-permute-start(bf16[256,1536]{1,0:T(8,128)(2,1)} %get-tuple-element.552), channel_id=1, source_target_pairs={{0,8},{4,12},{8,0},{12,4},{16,24},{20,28},{24,16},{28,20},{1,9},{5... | collective-permute-start | bytes 2359304 | tf_op jit(solution)/shard_map/ppermute | solution.py:111
  569.4 38.5 %collective-permute-start.70 = (bf16[256,1536]{1,0:T(8,128)(2,1)S(1)}, bf16[256,1536]{1,0:T(8,128)(2,1)S(1)}, u32[]{:S(2)}, u32[]{:S(2)}) collective-permute-start(bf16[256,1536]{1,0:T(8,128)(2,1)S(1)} %add_convert_fusion.3), channel_id=1, source_target_pairs={{0,16},{4,20},{8,24},{12,28},{16,0},{20,4},{24,8},{28,12},{1,17},{... | collective-permute-start | bytes 2359304 | tf_op jit(solution)/shard_map/ppermute | solution.py:111
  584.3 32.3 %collective-permute-start.74 = (bf16[256,512]{1,0:T(8,128)(2,1)}, bf16[256,512]{1,0:T(8,128)(2,1)S(1)}, u32[]{:S(2)}, u32[]{:S(2)}) collective-permute-start(bf16[256,512]{1,0:T(8,128)(2,1)} %get-tuple-element.567), channel_id=1, source_target_pairs={{0,8},{4,12},{8,0},{12,4},{16,24},{20,28},{24,16},{28,20},{1,9},{5... | collective-permute-start | bytes 786440 | tf_op jit(solution)/shard_map/ppermute | solution.py:111
  (110 other events, 1367.4 us)
